TPU v7x, 128 devices: a whole 4x4x4 slice. The times are simulated.
128 devices in a mesh: ctx: 16 (over z, y), fsdp: 8 (over x, core).
Axes of the slice: x: 4, y: 4, z: 4, core: 2. Of those that a mesh axis runs over, the one named last changes fastest.
Arguments:
- tokens: bfloat16 [24, 2048, 2048], P('fsdp', 'ctx'), may hold values from -6 to 6
- segment_ids: int32 [24, 2048], P('fsdp'), may hold values from 0 to 7, as said below
- end_rows: int32 [24, 8], P('fsdp'), may hold values from 0 to 2047, as said below
- input_norm_gain: float32 [2048], replicated, may hold values from 0.25 to 1.75
- query_weight: bfloat16 [2048, 1024], P(('ctx', 'fsdp')), may hold values from -1 to 1
- key_weight: bfloat16 [2048, 256], P(('ctx', 'fsdp')), may hold values from -1 to 1
- value_weight: bfloat16 [2048, 256], P(('ctx', 'fsdp')), may hold values from -0.125 to 0.125
- out_weight: bfloat16 [2048, 1024], P(('ctx', 'fsdp')), may hold values from -0.75 to 0.75
- head_weight: float32 [2048], replicated, may hold values from -0.125 to 0.125
- branch_grad: bfloat16 [24, 2048, 2048], P('fsdp', 'ctx'), may hold values from -6 to 6
Outputs:
- branch: bfloat16 [24, 2048, 2048], P('fsdp', 'ctx')
- rewards: float32 [24, 8], P('fsdp')
- grad_tokens: bfloat16 [24, 2048, 2048], P('fsdp', 'ctx')
- grad_query_weight: float32 [2048, 1024], P(('ctx', 'fsdp'))
- grad_key_weight: float32 [2048, 256], P(('ctx', 'fsdp'))
- grad_value_weight: float32 [2048, 256], P(('ctx', 'fsdp'))
- grad_out_weight: float32 [2048, 1024], P(('ctx', 'fsdp'))
Inputs may be any that keep to these rules, and one draw needn't show every extreme that they name: `segment_ids`: never falling along a slab; document d holds the positions after end_rows of d - 1 up to end_rows of d. `end_rows`: strictly rising within a slab; the last is always 2048 - 1.
All inputs are finite; a program needn't handle non-finite values.
Results may differ from a plain program's by a relative error of at most 0.03.
The roundings to bfloat16 on the way count: a program that leaves them out, or rounds other values in their place, can miss the bound.
Values may be sent and summed in bfloat16 or wider, within the bound.
No kernel may reach another device: no remote copies, remote signals or barrier semaphores. Data moves between devices by JAX's collectives and lax.ppermute only.
A program may use at most 192 MiB of HBM per device.

v0:
```python
import jax
import jax.numpy as jnp
from jax import lax
from jax.sharding import PartitionSpec as P

HEADS = 16
KV_HEADS = 4
HEAD_DIM = 64


eps = 1e-05
base_theta = 500000.0


def rotation_tables(first, count):
    half = HEAD_DIM // 2
    freqs = base_theta ** (-(2.0 * jnp.arange(half, dtype=jnp.float32)) / HEAD_DIM)
    angles = (first + jnp.arange(count, dtype=jnp.int32)).astype(jnp.float32)[:, None] * freqs[
        None, :
    ]
    return (jnp.cos(angles)[:, None, :], jnp.sin(angles)[:, None, :])


def rotate(values, cosine, sine):
    half = values.shape[-1] // 2
    front = values[..., :half]
    back = values[..., half:]
    return jnp.concatenate([front * cosine - back * sine, back * cosine + front * sine], -1)


def slab_pass(
    local, segments, ends, grad_out, input_norm_gain, head_weight, wq, wk, wv, wo, first_row, n_ctx
):
    group = HEADS // KV_HEADS
    scale = HEAD_DIM ** (-0.5)
    width = HEADS * HEAD_DIM
    tok_rows = local.shape[0]
    slab = tok_rows * n_ctx
    heads_here = HEADS // n_ctx
    block = min(512, slab)
    count_blocks = slab // block
    input_float = local.astype(jnp.float32)
    inverse_norm = lax.rsqrt(jnp.mean(input_float * input_float, -1, keepdims=True) + eps)
    centered_input = input_float * inverse_norm
    normalized_input = (centered_input * input_norm_gain).astype(jnp.bfloat16)
    cos_here, sin_here = rotation_tables(first_row, tok_rows)
    query = rotate(
        jnp.dot(normalized_input, wq, preferred_element_type=jnp.float32).reshape(
            tok_rows, HEADS, HEAD_DIM
        ),
        cos_here,
        sin_here,
    ).astype(jnp.bfloat16)
    keys = rotate(
        jnp.dot(normalized_input, wk, preferred_element_type=jnp.float32).reshape(
            tok_rows, KV_HEADS, HEAD_DIM
        ),
        cos_here,
        sin_here,
    ).astype(jnp.bfloat16)
    values = (
        jnp.dot(normalized_input, wv, preferred_element_type=jnp.float32)
        .astype(jnp.bfloat16)
        .reshape(tok_rows, KV_HEADS, HEAD_DIM)
    )
    keys = jnp.repeat(keys, group, axis=1).reshape(tok_rows, width)
    values = jnp.repeat(values, group, axis=1).reshape(tok_rows, width)
    query_all, key_all, value_all = (
        lax.all_to_all(
            query.reshape(tok_rows, width), "ctx", split_axis=1, concat_axis=0, tiled=True
        ),
        lax.all_to_all(keys, "ctx", split_axis=1, concat_axis=0, tiled=True),
        lax.all_to_all(values, "ctx", split_axis=1, concat_axis=0, tiled=True),
    )
    query_h = query_all.reshape(slab, heads_here, HEAD_DIM)
    key_h = key_all.reshape(slab, heads_here, HEAD_DIM)
    value_h = value_all.reshape(slab, heads_here, HEAD_DIM)
    place = jnp.arange(slab, dtype=jnp.int32)

    def block_probabilities(index):
        start = index * block
        rows = lax.dynamic_slice_in_dim(query_h, start, block, 0)
        rows_place = start + jnp.arange(block, dtype=jnp.int32)
        rows_segment = lax.dynamic_slice_in_dim(segments, start, block, 0)
        allowed = (place[None, :] <= rows_place[:, None]) & (
            segments[None, :] == rows_segment[:, None]
        )
        scores = jnp.einsum("qhd,khd->hqk", rows, key_h, preferred_element_type=jnp.float32) * scale
        scores = jnp.where(allowed[None], scores, -jnp.inf)
        top = jnp.max(scores, -1, keepdims=True)
        weights = jnp.exp(scores - top)
        return (rows, weights / jnp.sum(weights, -1, keepdims=True))

    def forward_block(index):
        rows, probs = block_probabilities(index)
        return jnp.einsum(
            "hqk,khd->qhd", probs.astype(jnp.bfloat16), value_h, preferred_element_type=jnp.float32
        ).astype(jnp.bfloat16)

    context_h = lax.map(forward_block, jnp.arange(count_blocks, dtype=jnp.int32)).reshape(
        slab, heads_here, HEAD_DIM
    )
    context_rows = lax.all_to_all(
        context_h.reshape(slab, heads_here * HEAD_DIM),
        "ctx",
        split_axis=0,
        concat_axis=1,
        tiled=True,
    )
    branch = jnp.dot(context_rows, wo.T, preferred_element_type=jnp.float32).astype(jnp.bfloat16)
    hidden = input_float + branch.astype(jnp.float32)
    marks = (ends[:, None] == (first_row + jnp.arange(tok_rows, dtype=jnp.int32))[None, :]).astype(
        jnp.float32
    )
    picked = jnp.dot(marks, hidden, precision=lax.Precision.HIGHEST)
    picked = picked * lax.rsqrt(jnp.mean(picked * picked, -1, keepdims=True) + eps)
    reward_part = jnp.sum(picked * head_weight, -1)
    context_grad = jnp.dot(grad_out, wo, preferred_element_type=jnp.float32).astype(jnp.bfloat16)
    grad_h = lax.all_to_all(context_grad, "ctx", split_axis=1, concat_axis=0, tiled=True).reshape(
        slab, heads_here, HEAD_DIM
    )

    def backward_block(carry, index):
        dk_total, dv_total = carry
        rows, probs = block_probabilities(index)
        start = index * block
        grad_rows = lax.dynamic_slice_in_dim(grad_h, start, block, 0)
        context_block = lax.dynamic_slice_in_dim(context_h, start, block, 0)
        dprobs = jnp.einsum("qhd,khd->hqk", grad_rows, value_h, preferred_element_type=jnp.float32)
        delta = jnp.sum(grad_rows.astype(jnp.float32) * context_block.astype(jnp.float32), -1)
        dscores = (probs * (dprobs - jnp.transpose(delta)[:, :, None])).astype(jnp.bfloat16)
        dq = jnp.einsum("hqk,khd->qhd", dscores, key_h, preferred_element_type=jnp.float32) * scale
        dk_total = (
            dk_total
            + jnp.einsum("hqk,qhd->khd", dscores, rows, preferred_element_type=jnp.float32) * scale
        )
        dv_total = dv_total + jnp.einsum(
            "hqk,qhd->khd",
            probs.astype(jnp.bfloat16),
            grad_rows,
            preferred_element_type=jnp.float32,
        )
        return ((dk_total, dv_total), dq)

    empty = jnp.zeros((slab, heads_here, HEAD_DIM), jnp.float32)
    (dk_all, dv_all), dq_blocks = lax.scan(
        backward_block, (empty, empty), jnp.arange(count_blocks, dtype=jnp.int32)
    )
    cos_all, sin_all = rotation_tables(0, slab)
    dq_h = rotate(dq_blocks.reshape(slab, heads_here, HEAD_DIM), cos_all, -sin_all).astype(
        jnp.bfloat16
    )
    dk_h = rotate(dk_all, cos_all, -sin_all).astype(jnp.bfloat16)
    dv_h = dv_all.astype(jnp.bfloat16)
    flat = heads_here * HEAD_DIM
    dquery, dkey_head, dvalue_head = (
        lax.all_to_all(dq_h.reshape(slab, flat), "ctx", split_axis=0, concat_axis=1, tiled=True),
        lax.all_to_all(dk_h.reshape(slab, flat), "ctx", split_axis=0, concat_axis=1, tiled=True),
        lax.all_to_all(dv_h.reshape(slab, flat), "ctx", split_axis=0, concat_axis=1, tiled=True),
    )
    dkey = (
        jnp.sum(dkey_head.astype(jnp.float32).reshape(tok_rows, KV_HEADS, group, HEAD_DIM), 2)
        .astype(jnp.bfloat16)
        .reshape(tok_rows, KV_HEADS * HEAD_DIM)
    )
    dvalue = (
        jnp.sum(dvalue_head.astype(jnp.float32).reshape(tok_rows, KV_HEADS, group, HEAD_DIM), 2)
        .astype(jnp.bfloat16)
        .reshape(tok_rows, KV_HEADS * HEAD_DIM)
    )
    dnormed = jnp.dot(dquery, wq.T, preferred_element_type=jnp.float32)
    dnormed = dnormed + jnp.dot(dkey, wk.T, preferred_element_type=jnp.float32)
    dnormed = dnormed + jnp.dot(dvalue, wv.T, preferred_element_type=jnp.float32)
    scaled_input = dnormed * input_norm_gain
    input_gradient = (
        inverse_norm
        * (
            scaled_input
            - centered_input * jnp.mean(scaled_input * centered_input, -1, keepdims=True)
        )
    ).astype(jnp.bfloat16)
    return (
        branch,
        reward_part,
        input_gradient,
        normalized_input,
        dquery,
        dkey,
        dvalue,
        context_rows,
    )


def on_device(
    tokens,
    segment_ids,
    end_rows,
    input_norm_gain,
    query_weight,
    key_weight,
    value_weight,
    out_weight,
    head_weight,
    branch_grad,
):
    n_ctx = lax.axis_size("ctx")
    rank = lax.axis_index("ctx")
    width = HEADS * HEAD_DIM
    slabs_here = tokens.shape[0]
    tok_rows = tokens.shape[1]
    first_row = rank * tok_rows
    wq, wk, wv, wo = (
        lax.all_gather(query_weight, ("ctx", "fsdp"), axis=0, tiled=True),
        lax.all_gather(key_weight, ("ctx", "fsdp"), axis=0, tiled=True),
        lax.all_gather(value_weight, ("ctx", "fsdp"), axis=0, tiled=True),
        lax.all_gather(out_weight, ("ctx", "fsdp"), axis=0, tiled=True),
    )
    branches, reward_parts, grads, normed_list, dq_list, dk_list, dv_list, context_list = (
        [],
        [],
        [],
        [],
        [],
        [],
        [],
        [],
    )
    for slab_index in range(slabs_here):
        result = slab_pass(
            tokens[slab_index],
            segment_ids[slab_index],
            end_rows[slab_index],
            branch_grad[slab_index],
            input_norm_gain,
            head_weight,
            wq,
            wk,
            wv,
            wo,
            first_row,
            n_ctx,
        )
        branches.append(result[0])
        reward_parts.append(result[1])
        grads.append(result[2])
        normed_list.append(result[3])
        dq_list.append(result[4])
        dk_list.append(result[5])
        dv_list.append(result[6])
        context_list.append(result[7])
    rewards = lax.psum(jnp.stack(reward_parts, 0), "ctx")
    normed_all = jnp.concatenate(normed_list, 0)
    dquery_all = jnp.concatenate(dq_list, 0)
    dkey_all = jnp.concatenate(dk_list, 0)
    dvalue_all = jnp.concatenate(dv_list, 0)
    context_all = jnp.concatenate(context_list, 0)
    grad_out_all = branch_grad.reshape(slabs_here * tok_rows, branch_grad.shape[2])
    summed = lax.psum_scatter(
        jnp.concatenate(
            [
                jnp.dot(normed_all.T, dquery_all, preferred_element_type=jnp.float32),
                jnp.dot(normed_all.T, dkey_all, preferred_element_type=jnp.float32),
                jnp.dot(normed_all.T, dvalue_all, preferred_element_type=jnp.float32),
                jnp.dot(grad_out_all.T, context_all, preferred_element_type=jnp.float32),
            ],
            1,
        ),
        ("ctx", "fsdp"),
        scatter_dimension=0,
        tiled=True,
    )
    kv_width = KV_HEADS * HEAD_DIM
    grad_q = summed[:, :width]
    grad_k = summed[:, width : width + kv_width]
    grad_v = summed[:, width + kv_width : width + 2 * kv_width]
    grad_o = summed[:, width + 2 * kv_width :]
    return (jnp.stack(branches, 0), rewards, jnp.stack(grads, 0), grad_q, grad_k, grad_v, grad_o)


def solution(mesh):
    placed = (
        P("fsdp", "ctx", None),
        P("fsdp", None),
        P("fsdp", None),
        P(),
        P(("ctx", "fsdp"), None),
        P(("ctx", "fsdp"), None),
        P(("ctx", "fsdp"), None),
        P(("ctx", "fsdp"), None),
        P(),
        P("fsdp", "ctx", None),
    )
    return jax.shard_map(
        on_device,
        mesh=mesh,
        in_specs=placed,
        out_specs=(
            P("fsdp", "ctx", None),
            P("fsdp", None),
            P("fsdp", "ctx", None),
            P(("ctx", "fsdp"), None),
            P(("ctx", "fsdp"), None),
            P(("ctx", "fsdp"), None),
            P(("ctx", "fsdp"), None),
        ),
        check_vma=False,
    )
```

profile of v0, /device:TPU:0, one launch (start us, length us, event | category | flops | bytes accessed | tf_op | source)
XLA Modules:
  0.0 1491.1 jit_solution(14116462618552623378)
XLA Ops:
  12.7 64.1 %all-gather.9.cloned.1.call-done = bf16[2048,256]{1,0:T(8,128)(2,1)} async-done(((bf16[16,256]{1,0:T(8,128)(2,1)}), bf16[2048,256]{1,0:T(8,128)(2,1)}) %all-gather.9.cloned.1.call-update) | async-done | bytes 1048592 | tf_op jit(solution)/shard_map/all_gather | solution.py:215
  83.7 57.0 %all-gather.7.cloned.1.call-done = bf16[2048,256]{1,0:T(8,128)(2,1)} async-done(((bf16[16,256]{1,0:T(8,128)(2,1)}), bf16[2048,256]{1,0:T(8,128)(2,1)}) %all-gather.7.cloned.1.call-update) | async-done | bytes 1048592 | tf_op jit(solution)/shard_map/all_gather | solution.py:214
  143.2 65.0 %all-gather.11.cloned.1.call-done = bf16[2048,1024]{1,0:T(8,128)(2,1)} async-done(((bf16[16,1024]{1,0:T(8,128)(2,1)}), bf16[2048,1024]{1,0:T(8,128)(2,1)}) %all-gather.11.cloned.1.call-update) | async-done | bytes 4194320 | tf_op jit(solution)/shard_map/all_gather | solution.py:216
  212.2 63.4 %all-gather.5.cloned.1.call-done = bf16[2048,1024]{1,0:T(8,128)(2,1)} async-done(((bf16[16,1024]{1,0:T(8,128)(2,1)}), bf16[2048,1024]{1,0:T(8,128)(2,1)}) %all-gather.5.cloned.1.call-update) | async-done | bytes 4194320 | tf_op jit(solution)/shard_map/all_gather | solution.py:213
  275.6 6.5 copy.173
  290.9 5.6 all-to-all-done.1
  300.8 7.8 all-to-all-done.12
  321.5 17.6 %while.78 = (s32[]{:T(128)}, bf16[4,512,1,64]{1,3,2,0:T(8,128)(2,1)S(1)}, s32[4]{0:T(128)S(1)}, s32[1,2048]{1,0:T(1,128)S(1)}, s32[2048]{0:T(1024)S(1)}, /*index...) while((s32[]{:T(128)}, ...), condition=%wide.region_4.5_spmd.clone, body=%wide.region_1.4_spmd.clone.sunk | while | flops 280002048 | bytes 14315747 | solution.py:100
  339.9 50.1 %while.81 = (s32[]{:T(128)}, f32[2048,1,64]{0,2,1:T(8,128)S(1)}, f32[2048,1,64]{0,2,1:T(8,128)}, f32[4,512,1,64]{1,0,3,2:T(4,128)S(1)}, s32[4]{0:T(128)S(1)}, /*...) while((s32[]{:T(128)}, f32[2048,1,64]{0,2,1:T(8,128)S(1)}, ...), condition=%wide.region_26.27_spmd.clone, body=%wide.region_22.26_spmd.clone.sunk | while | flops 688684032 | bytes 29135160 | solution.py:146
  408.1 4.7 all-to-all-start.15
  421.6 6.2 all-to-all-start.13
  454.0 7.3 all-to-all-start.16
  491.6 5.9 all-to-all-done.6
  527.5 17.6 %while.79 = (s32[]{:T(128)}, bf16[4,512,1,64]{1,3,2,0:T(8,128)(2,1)S(1)}, s32[4]{0:T(128)S(1)}, s32[1,2048]{1,0:T(1,128)S(1)}, s32[2048]{0:T(1024)S(1)}, /*index...) while((s32[]{:T(128)}, ...), condition=%wide.region_9.10_spmd.clone, body=%wide.region_6.9_spmd.clone.sunk | while | flops 280002048 | bytes 13267143 | solution.py:100
  545.1 7.3 all-to-all-start.8
  552.6 39.9 %while.82 = (s32[]{:T(128)}, f32[2048,1,64]{0,2,1:T(8,128)S(1)}, f32[2048,1,64]{0,2,1:T(8,128)}, f32[4,512,1,64]{1,0,3,2:T(4,128)S(1)}, s32[4]{0:T(128)S(1)}, /*...) while((s32[]{:T(128)}, f32[2048,1,64]{0,2,1:T(8,128)S(1)}, ...), condition=%wide.region_34.35_spmd.clone, body=%wide.region_30.34_spmd.clone.sunk | while | flops 688684032 | bytes 28086556 | solution.py:146
  593.1 7.4 all-to-all-start.3
  601.8 17.6 %while.80 = (s32[]{:T(128)}, bf16[4,512,1,64]{1,3,2,0:T(8,128)(2,1)S(1)}, s32[4]{0:T(128)S(1)}, s32[1,2048]{1,0:T(1,128)S(1)}, s32[2048]{0:T(1024)S(1)}, /*index...) while((s32[]{:T(128)}, ...), condition=%wide.region_14.15_spmd.clone, body=%wide.region_11.14_spmd.clone.sunk | while | flops 280002048 | bytes 13267143 | solution.py:100
  622.7 7.4 all-to-all-start.19
  630.2 43.3 %while.83 = (s32[]{:T(128)}, f32[2048,1,64]{0,2,1:T(8,128)S(1)}, f32[2048,1,64]{0,2,1:T(8,128)}, f32[4,512,1,64]{1,0,3,2:T(4,128)S(1)}, s32[4]{0:T(128)S(1)}, /*...) while((s32[]{:T(128)}, f32[2048,1,64]{0,2,1:T(8,128)S(1)}, ...), condition=%wide.region_42.43_spmd.clone, body=%wide.region_38.0_spmd.clone.sunk | while | flops 688684032 | bytes 29135160 | solution.py:146
  676.1 7.2 all-to-all-start.7
  687.2 4.8 all-to-all-done.7
  696.4 7.8 all-to-all-done.17
  717.2 6.4 all-to-all-start.18
  724.7 7.7 all-to-all-done.18
  738.8 5.7 all-to-all-done.23
  750.3 6.5 all-to-all-done.21
  761.0 6.9 fusion.174
  773.8 15.5 %pad_maximum_fusion = f32[2048,2560]{0,1:T(8,128)} fusion(f32[2048,1024]{0,1:T(8,128)S(1)} %convolution_bitcast_fusion.3, f32[2048,256]{0,1:T(8,128)} %fusion.255, f32[2048,256]{0,1:T(8,128)S(1)} %copy-done.31, f32[2048,1024]{0,1:T(8,128)S(1)} %copy-done.6), kind=kLoop, calls=%fused_computation.150 | loop fusion | flops 15728640 | bytes 41943040 | tf_op jit(solution)/shard_map/concatenate | solution.py:259
  789.3 20.0 %copy.234 = f32[2048,2560]{1,0:T(8,128)} copy(f32[2048,2560]{0,1:T(8,128)} %pad_maximum_fusion) | data formatting | bytes 41943040
  821.2 39.7 %psum.7 = f32[3,8]{1,0:T(4,128)} all-reduce(f32[3,8]{1,0:T(4,128)S(1)} %pad_maximum_fusion.16), channel_id=1, replica_groups=mesh['ctx'=16,'fsdp'=8] {'ctx'}, use_global_device_ids=true, to_apply=%region_21.22 | all-reduce | flops 24 | bytes 192 | tf_op jit(solution)/shard_map/psum | solution.py:251
  871.1 610.4 %reduce-scatter.4.cloned.1.call-done = f32[16,2560]{1,0:T(8,128)} async-done(((f32[2048,2560]{1,0:T(8,128)}), f32[16,2560]{1,0:T(8,128)}) %reduce-scatter.4.cloned.1.call-update) | async-done | bytes 163856
  (632 shorter events, 404.2 us)
Async XLA Ops:
  7.2 69.7 %all-gather.9.cloned.1.call-start = ((), (), s32[]{:S(2)}) async-start(), calls=%async_computation.27 | async-start | bytes 1056768 | tf_op jit(solution)/shard_map/all_gather | solution.py:215
  7.9 132.8 %all-gather.7.cloned.1.call-start = ((), (), s32[]{:S(2)}) async-start(), calls=%async_computation.26 | async-start | bytes 1056768 | tf_op jit(solution)/shard_map/all_gather | solution.py:214
  8.7 199.6 %all-gather.11.cloned.1.call-start = ((), (), s32[]{:S(2)}) async-start(), calls=%async_computation.28 | async-start | bytes 4227072 | tf_op jit(solution)/shard_map/all_gather | solution.py:216
  9.4 266.2 %all-gather.5.cloned.1.call-start = ((), (), s32[]{:S(2)}) async-start(), calls=%async_computation.25 | async-start | bytes 4227072 | tf_op jit(solution)/shard_map/all_gather | solution.py:213
  11.3 276.1 %copy-start.72 = (f32[128]{0:T(128)}, f32[128]{0:T(128)S(1)}, u32[]{:S(2)}) copy-start(f32[128]{0:T(128)S(1)} %add_rsqrt_fusion.5) | copy-start | bytes 1540
  11.4 288.6 %copy-start.45 = (f32[128,32]{0,1:T(8,128)}, f32[128,32]{0,1:T(8,128)S(1)}, u32[]{:S(2)}) copy-start(f32[128,32]{0,1:T(8,128)S(1)} %get-tuple-element.770) | copy-start | bytes 49156
  11.4 288.6 %copy-start.47 = (f32[128,32]{0,1:T(8,128)}, f32[128,32]{0,1:T(8,128)S(1)}, u32[]{:S(2)}) copy-start(f32[128,32]{0,1:T(8,128)S(1)} %get-tuple-element.771) | copy-start | bytes 49156
  79.3 202.8 %all-to-all-start.2 = ((bf16[128,16,64]{0,2,1:T(8,128)(2,1)}), bf16[128,16,64]{0,2,1:T(8,128)(2,1)S(1)}, u32[]{:S(2)}, u32[]{:S(2)}) async-start(bf16[128,16,64]{0,2,1:T(8,128)(2,1)} %bitcast.12), calls=%async_computation.2 | async-start | bytes 524288 | tf_op jit(solution)/shard_map/all_to_all | solution.py:73
  282.8 13.6 all-to-all-start.1
  296.4 12.2 all-to-all-start.12
  308.6 12.5 all-to-all-start
  394.9 12.5 all-to-all-start.14
  408.1 13.4 all-to-all-start.15
  421.6 14.9 all-to-all-start.13
  436.5 17.5 %all-to-all-start.20 = ((bf16[128,16,64]{0,2,1:T(8,128)(2,1)}), bf16[128,16,64]{0,2,1:T(8,128)(2,1)}, u32[]{:S(2)}, u32[]{:S(2)}) async-start(bf16[128,16,64]{0,2,1:T(8,128)(2,1)} %bitcast.74), calls=%async_computation.20 | async-start | bytes 524288 | tf_op jit(solution)/shard_map/all_to_all | solution.py:119
  454.0 16.0 %all-to-all-start.16 = ((bf16[128,16,64]{0,2,1:T(8,128)(2,1)}), bf16[128,16,64]{0,2,1:T(8,128)(2,1)}, u32[]{:S(2)}, u32[]{:S(2)}) async-start(bf16[128,16,64]{0,2,1:T(8,128)(2,1)} %bitcast.754), calls=%async_computation.16 | async-start | bytes 524288 | tf_op jit(solution)/shard_map/all_to_all | solution.py:119
  471.6 12.9 all-to-all-start.5
  485.2 12.3 all-to-all-start.6
  497.5 12.2 all-to-all-start.4
  510.5 12.4 all-to-all-start.9
  523.7 21.4 %all-to-all-start.10 = ((bf16[128,16,64]{0,2,1:T(8,128)(2,1)}), bf16[128,16,64]{0,2,1:T(8,128)(2,1)S(1)}, u32[]{:S(2)}, u32[]{:S(2)}) async-start(bf16[128,16,64]{0,2,1:T(8,128)(2,1)} %bitcast.38), calls=%async_computation.10 | async-start | bytes 524288 | tf_op jit(solution)/shard_map/all_to_all | solution.py:73
  545.1 47.9 %all-to-all-start.8 = ((bf16[128,16,64]{0,2,1:T(8,128)(2,1)}), bf16[128,16,64]{0,2,1:T(8,128)(2,1)}, u32[]{:S(2)}, u32[]{:S(2)}) async-start(bf16[128,16,64]{0,2,1:T(8,128)(2,1)} %pad_maximum_fusion.6), calls=%async_computation.8 | async-start | bytes 524288 | tf_op jit(solution)/shard_map/all_to_all | solution.py:69
  593.1 29.6 %all-to-all-start.3 = ((bf16[16,128,64]{1,2,0:T(8,128)(2,1)}), bf16[16,128,64]{1,2,0:T(8,128)(2,1)S(1)}, u32[]{:S(2)}, u32[]{:S(2)}) async-start(bf16[16,128,64]{1,2,0:T(8,128)(2,1)} %copy.180), calls=%async_computation.3 | async-start | bytes 524288 | tf_op jit(solution)/shard_map/all_to_all | solution.py:103
  622.7 53.4 %all-to-all-start.19 = ((bf16[16,128,64]{1,2,0:T(8,128)(2,1)}), bf16[16,128,64]{1,2,0:T(8,128)(2,1)}, u32[]{:S(2)}, u32[]{:S(2)}) async-start(bf16[16,128,64]{1,2,0:T(8,128)(2,1)} %copy.214), calls=%async_computation.19 | async-start | bytes 524288 | tf_op jit(solution)/shard_map/all_to_all | solution.py:159
  676.1 15.9 %all-to-all-start.7 = ((bf16[16,128,64]{1,2,0:T(8,128)(2,1)}), bf16[16,128,64]{1,2,0:T(8,128)(2,1)S(1)}, u32[]{:S(2)}, u32[]{:S(2)}) async-start(bf16[16,128,64]{1,2,0:T(8,128)(2,1)} %copy.186), calls=%async_computation.7 | async-start | bytes 524288 | tf_op jit(solution)/shard_map/all_to_all | solution.py:103
  692.0 12.2 all-to-all-start.17
  704.2 13.1 all-to-all-start.22
  717.2 15.1 %all-to-all-start.18 = ((bf16[16,128,64]{1,2,0:T(8,128)(2,1)}), bf16[16,128,64]{1,2,0:T(8,128)(2,1)S(1)}, u32[]{:S(2)}, u32[]{:S(2)}) async-start(bf16[16,128,64]{1,2,0:T(8,128)(2,1)} %pad_maximum_fusion.10), calls=%async_computation.18 | async-start | bytes 524288 | tf_op jit(solution)/shard_map/all_to_all | solution.py:158
  732.3 12.2 all-to-all-start.23
  744.5 12.2 all-to-all-start.21
  756.7 12.9 all-to-all-start.11
  760.9 720.5 %reduce-scatter.4.cloned.1.call-start = ((), (), s32[]{:S(2)}) async-start(), calls=%async_computation.29 | async-start | bytes 21135360
  (94 other events, 1571.8 us)
Sparse Core Ops, SparseCore 0:
  10.8 65.9 all-gather.8
  79.6 61.0 all-gather.6
  143.8 64.3 all-gather.10
  211.2 64.3 all-gather.4
  809.4 672.0 reduce-scatter.3
where the time goes:
time: 1500 us; the launch traced here: 1490 us
  waiting for transfers between devices  945 us (63%)
  matrix products  180 us (12%)
  starting transfers between devices  116 us (8%)
  local copies, waits for them, and re-layouts  106 us (7%)
  other arithmetic  72.4 us (5%)
  blocking collectives  39.7 us (3%)
  loops' own time  17 us (1%)
  between operations  15.8 us (1%)
    unnamed x6, waiting for transfers between devices  613 us
    all_gather x1, waiting for transfers between devices, on_device(): lax.all_gather(out_weight, ('ctx', 'fsdp'), axis=0, tiled=True)  65 us
    all_gather x1, waiting for transfers between devices, on_device(): lax.all_gather(value_weight, ('ctx', 'fsdp'), axis=0, tiled=True)  64.1 us
    all_gather x1, waiting for transfers between devices, on_device(): lax.all_gather(query_weight, ('ctx', 'fsdp'), axis=0, tiled=True)  63.4 us
    all_gather x1, waiting for transfers between devices, on_device(): lax.all_gather(key_weight, ('ctx', 'fsdp'), axis=0, tiled=True)  57 us
    psum x1, blocking collectives, on_device(): rewards = lax.psum(jnp.stack(reward_parts, 0), 'ctx')  39.7 us
    dot_general x24, matrix products, block_probabilities(): jnp.einsum('qhd,khd->hqk', rows, key_h, preferred_element_type=jnp.float32)  34.5 us
    dot_general x12, matrix products, backward_block(): jnp.einsum('hqk,qhd->khd', probs.astype(jnp.bfloat16), grad_rows, preferr...  31.1 us
  transfers between devices with their start and end apart: 29, of which 23 were waited for; matrix products, arithmetic and copies ran while one was open for 16% of the time, Pallas kernels for 0%

commit v1 on v0

v1 whole, which is shorter than its diff:
```python
import jax
import jax.numpy as jnp
from jax import lax
from jax.experimental import pallas as pl
from jax.experimental.pallas import tpu as pltpu
from jax.sharding import Mesh
from jax.sharding import PartitionSpec as P

HEADS = 16
KV_HEADS = 4
HEAD_DIM = 64
GROUP = HEADS // KV_HEADS
HALF = HEAD_DIM // 2
BLOCK = 256

eps = 1e-05
base_theta = 500000.0


def rotation_tables(positions):
    freqs = base_theta ** (-(2.0 * jnp.arange(HALF, dtype=jnp.float32)) / HEAD_DIM)
    angles = positions.astype(jnp.float32)[None, :] * freqs[:, None]
    return jnp.cos(angles), jnp.sin(angles)


def attention_kernel(
    ends_ref, in_ref, cos_ref, sin_ref, out_ref, kt_s, k_s, vt_s, v_s, p_s, dk_s, dv_s
):
    slab = pl.program_id(0)
    n_src, _, rows = in_ref.shape
    per = BLOCK // rows
    blocks = n_src // per
    docs = ends_ref.shape[1]
    f32, bf16 = jnp.float32, jnp.bfloat16
    hd = HEAD_DIM

    def load(b, part):
        return jnp.concatenate(
            [in_ref[b * per + r, part * hd : (part + 1) * hd, :] for r in range(per)], axis=1
        )

    for b in range(blocks):
        kt = load(b, 1)
        vt = load(b, 2)
        kt_s[b] = kt
        vt_s[b] = vt
        k_s[b] = kt.T
        v_s[b] = vt.T
    dk_s[...] = jnp.zeros_like(dk_s)
    dv_s[...] = jnp.zeros_like(dv_s)

    key_iota = lax.broadcasted_iota(jnp.int32, (BLOCK, BLOCK), 0)
    row_iota = lax.broadcasted_iota(jnp.int32, (1, BLOCK), 1)

    for i in range(blocks):
        qt = load(i, 0)
        dot_t = load(i, 3)
        place = row_iota + i * BLOCK
        start = jnp.zeros((1, BLOCK), jnp.int32)
        first = jnp.int32(0)
        for d in range(docs - 1):
            after = ends_ref[slab, d] + 1
            start = jnp.where(place >= after, after, start)
            first = jnp.where(after <= i * BLOCK, after, first)
        lo = lax.shift_right_logical(first, BLOCK.bit_length() - 1)

        def scores(j, top, qt=qt, place=place, start=start):
            s = jnp.dot(k_s[j], qt, preferred_element_type=f32)
            at = key_iota + j * BLOCK
            s = jnp.where((at >= start) & (at <= place), s, -jnp.inf)
            p_s[j] = s
            return jnp.maximum(top, jnp.max(s, axis=0, keepdims=True))

        top = scores(i, jnp.full((1, BLOCK), -jnp.inf, f32))
        top = lax.fori_loop(lo, i, scores, top)

        def forward(j, carry, top=top):
            total, acc = carry
            w = jnp.exp(p_s[j] - top)
            p_s[j] = w
            total = total + jnp.sum(w, axis=0, keepdims=True)
            acc = acc + jnp.dot(vt_s[j], w.astype(bf16), preferred_element_type=f32)
            return total, acc

        carry = forward(i, (jnp.zeros((1, BLOCK), f32), jnp.zeros((hd, BLOCK), f32)))
        total, acc = lax.fori_loop(lo, i, forward, carry)
        inv = 1.0 / total
        ctx = (acc * inv).astype(bf16)
        delta = jnp.sum(dot_t.astype(f32) * ctx.astype(f32), axis=0, keepdims=True)

        def backward(j, dq, qt=qt, dot_t=dot_t, inv=inv, delta=delta):
            probs = p_s[j] * inv
            dp = jnp.dot(v_s[j], dot_t, preferred_element_type=f32)
            ds = (probs * (dp - delta)).astype(bf16)
            trans = (((1,), (1,)), ((), ()))
            dv_s[j] += lax.dot_general(
                dot_t, probs.astype(bf16), trans, preferred_element_type=f32
            )
            dk_s[j] += lax.dot_general(qt, ds, trans, preferred_element_type=f32)
            return dq + jnp.dot(kt_s[j], ds, preferred_element_type=f32)

        dq = backward(i, jnp.zeros((hd, BLOCK), f32))
        dq = lax.fori_loop(lo, i, backward, dq) * (hd**-0.5)
        for r in range(per):
            at = slice(r * rows, (r + 1) * rows)
            src = i * per + r
            out_ref[src, 0:hd, :] = ctx[:, at]
            a, b = dq[:HALF, at], dq[HALF:, at]
            cosine, sine = cos_ref[src], sin_ref[src]
            out_ref[src, hd : hd + HALF, :] = (a * cosine + b * sine).astype(bf16)
            out_ref[src, hd + HALF : 2 * hd, :] = (b * cosine - a * sine).astype(bf16)

    for j in range(blocks):
        for r in range(per):
            at = slice(r * rows, (r + 1) * rows)
            src = j * per + r
            a, b = dk_s[j, :HALF, at], dk_s[j, HALF:, at]
            cosine, sine = cos_ref[src], sin_ref[src]
            out_ref[src, 2 * hd : 2 * hd + HALF, :] = (a * cosine + b * sine).astype(bf16)
            out_ref[src, 2 * hd + HALF : 3 * hd, :] = (b * cosine - a * sine).astype(bf16)
            out_ref[src, 3 * hd : 4 * hd, :] = dv_s[j, :, at].astype(bf16)


def attention(received, ends, cos_all, sin_all):
    n_src, width, tok = received.shape
    slabs = ends.shape[0]
    rows = tok // slabs
    blocks = n_src * rows // BLOCK
    bf16, f32 = jnp.bfloat16, jnp.float32
    table = pl.BlockSpec((n_src, HALF, rows), lambda s, e: (0, 0, 0))
    part = pl.BlockSpec((n_src, width, rows), lambda s, e: (0, 0, s))
    return pl.pallas_call(
        attention_kernel,
        out_shape=jax.ShapeDtypeStruct(received.shape, bf16),
        grid_spec=pltpu.PrefetchScalarGridSpec(
            num_scalar_prefetch=1,
            grid=(slabs,),
            in_specs=[part, table, table],
            out_specs=part,
            scratch_shapes=[
                pltpu.VMEM((blocks, HEAD_DIM, BLOCK), bf16),
                pltpu.VMEM((blocks, BLOCK, HEAD_DIM), bf16),
                pltpu.VMEM((blocks, HEAD_DIM, BLOCK), bf16),
                pltpu.VMEM((blocks, BLOCK, HEAD_DIM), bf16),
                pltpu.VMEM((blocks, BLOCK, BLOCK), f32),
                pltpu.VMEM((blocks, HEAD_DIM, BLOCK), f32),
                pltpu.VMEM((blocks, HEAD_DIM, BLOCK), f32),
            ],
        ),
        compiler_params=pltpu.CompilerParams(vmem_limit_bytes=40 * 1024 * 1024),
        cost_estimate=pl.CostEstimate(
            flops=20 * 10**9, bytes_accessed=6 * 2**20, transcendentals=3 * 2**20
        ),
        name="attention",
    )(ends, received, cos_all, sin_all)


def on_device(
    tokens,
    segment_ids,
    end_rows,
    input_norm_gain,
    query_weight,
    key_weight,
    value_weight,
    out_weight,
    head_weight,
    branch_grad,
):
    del segment_ids
    bf16, f32 = jnp.bfloat16, jnp.float32
    n_ctx, n_x, n_core = (lax.axis_size(a) for a in ("ctx", "x", "core"))
    rank = lax.axis_index("ctx")
    core = lax.axis_index("core")
    slabs, rows, model = tokens.shape
    docs = end_rows.shape[1]
    tok = slabs * rows
    width = HEADS * HEAD_DIM
    kv_width = KV_HEADS * HEAD_DIM
    qkv = width + 2 * kv_width
    swap = [(c, n_core - 1 - c) for c in range(n_core)]

    weights = lax.all_gather(
        jnp.concatenate([query_weight, key_weight, value_weight, out_weight], 1),
        ("ctx", "x", "core"),
        axis=0,
        tiled=True,
    )

    flat = tokens.reshape(tok, model)
    grad_out = branch_grad.reshape(tok, model)
    wide = flat.astype(f32)
    inverse_norm = lax.rsqrt(jnp.mean(wide * wide, -1, keepdims=True) + eps)
    normed = (wide * inverse_norm * input_norm_gain).astype(bf16)

    def by_core(values):
        split = values.T.reshape(model // (16 * n_core), n_core, 16, tok)
        mine = lax.dynamic_index_in_dim(split, core, 1, keepdims=False).reshape(-1, tok)
        other = lax.dynamic_index_in_dim(split, 1 - core, 1, keepdims=False).reshape(-1, tok)
        return mine, lax.ppermute(other, "core", swap)

    normed_mine, normed_other = by_core(normed)
    grad_out_mine, grad_out_other = by_core(grad_out)

    first = rank * rows
    cos_all, sin_all = rotation_tables(jnp.arange(n_ctx * rows, dtype=jnp.int32))
    cos_here, sin_here = rotation_tables(first + jnp.arange(rows, dtype=jnp.int32))
    cos_here = jnp.tile(cos_here, (1, slabs))[None]
    sin_here = jnp.tile(sin_here, (1, slabs))[None]
    over = (((0,), (1,)), ((), ()))
    projected = lax.dot_general(weights[:, :qkv], normed, over, preferred_element_type=f32)
    turning = projected[: width + kv_width].reshape(HEADS + KV_HEADS, 2, HALF, tok)
    front, back = turning[:, 0], turning[:, 1]
    turned = jnp.concatenate(
        [front * cos_here - back * sin_here, back * cos_here + front * sin_here], 1
    )
    query = (turned[:HEADS] * (HEAD_DIM**-0.5)).astype(bf16)
    keys = jnp.repeat(turned[HEADS:].astype(bf16), GROUP, axis=0)
    values = projected[width + kv_width :].astype(bf16).reshape(KV_HEADS, HEAD_DIM, tok)
    values = jnp.repeat(values, GROUP, axis=0)
    context_grad = lax.dot_general(
        weights[:, qkv:], grad_out, over, preferred_element_type=f32
    ).astype(bf16)
    send = jnp.concatenate(
        [query, keys, values, context_grad.reshape(HEADS, HEAD_DIM, tok)], 1
    )
    received = lax.all_to_all(send, "ctx", split_axis=0, concat_axis=0, tiled=True)

    def by_source(table):
        return jnp.swapaxes(table.reshape(HALF, n_ctx, rows), 0, 1)

    results = attention(received, end_rows, by_source(cos_all), by_source(sin_all))
    back_home = lax.all_to_all(results, "ctx", split_axis=0, concat_axis=0, tiled=True)

    hd = HEAD_DIM
    context = back_home[:, :hd].reshape(width, tok)
    dquery = back_home[:, hd : 2 * hd].reshape(width, tok)

    def over_group(heads):
        heads = heads.astype(f32).reshape(KV_HEADS, GROUP, hd, tok)
        return jnp.sum(heads, 1).astype(bf16).reshape(kv_width, tok)

    dkey = over_group(back_home[:, 2 * hd : 3 * hd])
    dvalue = over_group(back_home[:, 3 * hd :])
    grads = jnp.concatenate([dquery, dkey, dvalue], 0)
    sent = lax.ppermute(jnp.concatenate([grads, context], 0), "core", swap)

    last = (((1,), (1,)), ((), ()))

    def two(a, b, c, d):
        return lax.dot_general(
            jnp.concatenate([a, c], 1),
            jnp.concatenate([b, d], 1),
            last,
            preferred_element_type=f32,
        ).astype(bf16)

    partial = jnp.concatenate(
        [
            two(normed_mine, grads, normed_other, sent[:qkv]),
            two(grad_out_mine, context, grad_out_other, sent[qkv:]),
        ],
        1,
    )
    summed = lax.psum_scatter(partial, "ctx", scatter_dimension=0, tiled=True)
    pieces = lax.all_to_all(summed, "x", split_axis=0, concat_axis=0, tiled=True)
    summed = jnp.sum(pieces.astype(f32).reshape(n_x, -1, qkv + width), 0)

    branch = lax.dot_general(context, weights[:, qkv:], over, preferred_element_type=f32)
    branch = branch.astype(bf16)
    here = jnp.arange(slabs, dtype=jnp.int32)
    marks = (
        (end_rows[:, :, None, None] == first + jnp.arange(rows, dtype=jnp.int32))
        & (here[:, None, None, None] == here[:, None])
    ).astype(bf16)
    marks = marks.reshape(slabs * docs, tok)
    picked = jnp.dot(marks, flat, preferred_element_type=f32) + jnp.dot(
        marks, branch, preferred_element_type=f32
    )
    picked = picked * lax.rsqrt(jnp.mean(picked * picked, -1, keepdims=True) + eps)
    rewards = jnp.sum(picked * head_weight, -1).reshape(slabs, docs)
    step = 1
    while step < n_ctx:
        pairs = [(c, c ^ step) for c in range(n_ctx)]
        rewards = rewards + lax.ppermute(rewards, "ctx", pairs)
        step *= 2

    dnormed = lax.dot_general(grads, weights[:, :qkv], over, preferred_element_type=f32)
    scaled = dnormed * input_norm_gain
    centered = wide * inverse_norm
    grad_tokens = inverse_norm * (
        scaled - centered * jnp.mean(scaled * centered, -1, keepdims=True)
    )
    return (
        branch.reshape(tokens.shape),
        rewards,
        grad_tokens.astype(bf16).reshape(tokens.shape),
        summed[:, :width],
        summed[:, width : width + kv_width],
        summed[:, width + kv_width : qkv],
        summed[:, qkv:],
    )


def solution(mesh):
    n_ctx, n_fsdp = mesh.devices.shape
    chips = Mesh(mesh.devices.reshape(n_ctx, n_fsdp // 2, 2), ("ctx", "x", "core"))
    fsdp = ("x", "core")
    rows = P(("ctx", "x", "core"), None)
    acts = P(fsdp, "ctx", None)
    return jax.shard_map(
        on_device,
        mesh=chips,
        in_specs=(
            acts,
            P(fsdp, None),
            P(fsdp, None),
            P(),
            rows,
            rows,
            rows,
            rows,
            P(),
            acts,
        ),
        out_specs=(acts, P(fsdp, None), acts, rows, rows, rows, rows),
        check_vma=False,
    )
```

time: 1500 us -> 391 us (0.26)
  waiting for transfers between devices: 945 us -> 245 us
  matrix products: 180 us -> 31.9 us
  starting transfers between devices: 116 us -> 22.5 us
  local copies, waits for them, and re-layouts: 106 us -> 16.3 us
  other arithmetic: 72.4 us -> 17.6 us
  Pallas kernels: 0 us -> 42.1 us
  blocking collectives: 39.7 us -> 0 us
  loops' own time: 17 us -> 0 us
    unnamed x6 -> x2, waiting for transfers between devices: 613 us -> 0.03 us
    all_gather x4 -> x1, waiting for transfers between devices: 250 us -> 75.1 us  [on_device(): lax.all_gather(jnp.concatenate([query_weight, key_weight, value_weight, o...]
    dot_general x115 -> x8, matrix products: 180 us -> 31.9 us  [the longest x2 10.1 us: two(): lax.dot_general(jnp.concatenate([a, c], 1), jnp.concatenate([b, d], 1), l...]
    all_to_all x24 -> x3, starting transfers between devices: 115 us -> 14 us  [the longest x1 5.34 us: on_device(): lax.all_to_all(send, 'ctx', split_axis=0, concat_axis=0, tiled=True)]
    reduce_scatter x0 -> x1, waiting for transfers between devices: none -> 80.7 us  [on_device(): summed = lax.psum_scatter(partial, 'ctx', scatter_dimension=0, tiled=True)]
    pallas_call x0 -> x1, Pallas kernels: none -> 42.1 us  [attention(): pl.pallas_call(attention_kernel, out_shape=jax.ShapeDtypeStruct(received....]
    psum x1 -> x0, blocking collectives: 39.7 us -> none  [on_device(): rewards = lax.psum(jnp.stack(reward_parts, 0), 'ctx')]
    reduce_sum x44 -> x4, other arithmetic: 29.1 us -> 4.39 us  [the longest x1 2.36 us: over_group(): return jnp.sum(heads, 1).astype(bf16).reshape(kv_width, tok)]
  transfers between devices with their start and end apart: 29 -> 12, of which waited for: 23 -> 8; matrix products, arithmetic and copies ran while one was open for 16% -> 9% of each run, Pallas kernels for 0% -> 0%
where the time goes in v1:
time: 391 us; the launch traced here: 390 us
  waiting for transfers between devices  245 us (63%)
  Pallas kernels  42.1 us (11%)
  matrix products  31.9 us (8%)
  starting transfers between devices  22.5 us (6%)
  other arithmetic  17.6 us (5%)
  local copies, waits for them, and re-layouts  16.3 us (4%)
  between operations  14.4 us (4%)
    reduce_scatter x1, waiting for transfers between devices, on_device(): summed = lax.psum_scatter(partial, 'ctx', scatter_dimension=0, tiled=True)  80.7 us
    all_gather x1, waiting for transfers between devices, on_device(): lax.all_gather(jnp.concatenate([query_weight, key_weight, value_weight, o...  75.1 us
    all_to_all x1, waiting for transfers between devices, on_device(): lax.all_to_all(send, 'ctx', split_axis=0, concat_axis=0, tiled=True)  46.9 us
    pallas_call x1, Pallas kernels, attention(): pl.pallas_call(attention_kernel, out_shape=jax.ShapeDtypeStruct(received....  42.1 us
    all_to_all x1, waiting for transfers between devices, on_device(): lax.all_to_all(results, 'ctx', split_axis=0, concat_axis=0, tiled=True)  33 us
    dot_general x2, matrix products, two(): lax.dot_general(jnp.concatenate([a, c], 1), jnp.concatenate([b, d], 1), l...  10.1 us
    ppermute x4, waiting for transfers between devices, on_device(): rewards = rewards + lax.ppermute(rewards, 'ctx', pairs)  9.49 us
    ppermute x4, starting transfers between devices, on_device(): rewards = rewards + lax.ppermute(rewards, 'ctx', pairs)  7.86 us
  transfers between devices with their start and end apart: 12, of which 8 were waited for; matrix products, arithmetic and copies ran while one was open for 9% of the time, Pallas kernels for 0%

profile of v1, /device:TPU:0, one launch (start us, length us, event | category | flops | bytes accessed | tf_op | source)
XLA Modules:
  0.0 390.0 jit_solution(285298900015087199)
XLA Ops:
  7.2 1.5 pad_maximum_fusion.4
  8.7 1.8 multiply_reduce_fusion.1
  10.7 75.1 %all-gather.2.cloned.1.call-done = bf16[2048,2560]{1,0:T(8,128)(2,1)} async-done(((bf16[16,2560]{1,0:T(8,128)(2,1)}), bf16[2048,2560]{1,0:T(8,128)(2,1)}) %all-gather.2.cloned.1.call-update) | async-done | bytes 10485776 | tf_op jit(solution)/shard_map/all_gather | solution.py:183
  85.8 6.2 %fusion.2 = f32[1536,384]{1,0:T(8,128)S(1)} fusion(bf16[2048,2560]{1,0:T(8,128)(2,1)} %all-gather.2.cloned.1.call-done, bf16[384,2048]{1,0:T(8,128)(2,1)} %bitcast.66, f32[2048]{0:T(1024)} %param.12, f32[384]{0:T(512)S(1)} %rsqrt_bitcast_fusion), kind=kOutput, calls=%fused_computation.2 | convolution fusion | flops 2419064832 | bytes 10233344 | tf_op jit(solution)/shard_map/dot_general | solution.py:211
  93.9 4.6 %fusion.33 = bf16[1024,384]{1,0:T(8,128)(2,1)S(1)} fusion(bf16[384,2048]{1,0:T(8,128)(2,1)S(1)} %bitcast.80, bf16[2048,2560]{1,0:T(8,128)(2,1)} %all-gather.2.cloned.1.call-done), kind=kOutput, calls=%fused_computation.42 | convolution fusion | flops 1611005952 | bytes 6553600 | tf_op jit(solution)/shard_map/dot_general | solution.py:221
  98.7 2.0 pad_maximum_fusion.1
  100.7 5.3 %all-to-all-start = ((bf16[16,256,384]{2,1,0:T(8,128)(2,1)}), bf16[16,256,384]{2,1,0:T(8,128)(2,1)S(1)}, u32[]{:S(2)}, u32[]{:S(2)}) async-start(bf16[16,256,384]{2,1,0:T(8,128)(2,1)} %pad_maximum_fusion.1), calls=%async_computation | async-start | bytes 6291456 | tf_op jit(solution)/shard_map/all_to_all | solution.py:227
  106.1 1.8 multiply_sine_fusion
  107.8 46.9 %all-to-all-done.in_ref = bf16[16,256,384]{2,1,0:T(8,128)(2,1)S(1)} async-done(((bf16[16,256,384]{2,1,0:T(8,128)(2,1)}), bf16[16,256,384]{2,1,0:T(8,128)(2,1)S(1)}, u32[]{:S(2)}, u32[]{:S(2)}) %all-to-all-start) | async-done | bytes 3145760 | tf_op jit(solution)/shard_map/all_to_all | solution.py:227
  155.7 42.1 %attention.1 = bf16[16,256,384]{2,1,0:T(8,128)(2,1)} custom-call(s32[3,8]{1,0:T(4,128)S(1)} %copy-done.1, bf16[16,256,384]{2,1,0:T(8,128)(2,1)S(1)} %all-to-all-done.in_ref, f32[16,32,128]{2,1,0:T(8,128)S(1)} %copy-done, f32[16,32,128]{2,1,0:T(8,128)S(1)} %get-tuple-element.23.sin_ref), custom_call_target="tpu_custom_call" | custom-call | flops 20000000000 | bytes 6291456 | tf_op jit(solution)/shard_map/attention/pallas_call | solution.py:132
  197.8 4.4 %all-to-all-start.1 = ((bf16[16,256,384]{2,1,0:T(8,128)(2,1)}), bf16[16,256,384]{2,1,0:T(8,128)(2,1)S(1)}, u32[]{:S(2)}, u32[]{:S(2)}) async-start(bf16[16,256,384]{2,1,0:T(8,128)(2,1)} %attention.1), calls=%async_computation.1 | async-start | bytes 6291456 | tf_op jit(solution)/shard_map/all_to_all | solution.py:233
  202.3 2.6 copy.25
  204.9 2.7 constant_dynamic-slice_fusion.1
  207.6 33.0 %all-to-all-done.1 = bf16[16,256,384]{2,1,0:T(8,128)(2,1)S(1)} async-done(((bf16[16,256,384]{2,1,0:T(8,128)(2,1)}), bf16[16,256,384]{2,1,0:T(8,128)(2,1)S(1)}, u32[]{:S(2)}, u32[]{:S(2)}) %all-to-all-start.1) | async-done | bytes 3145760 | tf_op jit(solution)/shard_map/all_to_all | solution.py:233
  240.6 1.6 copy-done.3
  242.4 2.4 bitcast_reduce_fusion.1
  244.8 1.5 pad_maximum_fusion.2
  246.3 6.1 %multiply_reduce_fusion = (f32[384]{0:T(512)S(1)}, f32[384,2048]{1,0:T(8,128)S(1)}) fusion(f32[384]{0:T(512)S(1)} %rsqrt_bitcast_fusion, bf16[3,128,2048]{2,1,0:T(8,128)(2,1)S(1)} %copy-done.2, f32[2048]{0:T(1024)S(1)} %copy-done.13, bf16[2048,2560]{1,0:T(8,128)(2,1)} %all-gather.2.cloned.1.call-done, bf16[256,384]{1,0:T(8,128)(2,1)S(1)} %bitcast.92, ...), kind=kOutput, calls=%fused_computation.12 | convolution fusion | flops 2423389696 | bytes 12200960 | tf_op jit(solution)/shard_map/dot_general | solution.py:288
  252.4 2.5 fusion.41
  254.9 1.9 copy.24
  260.2 3.0 convolution_convert_fusion.1
  263.3 7.0 %convolution_convert_fusion = bf16[1024,1536]{1,0:T(8,128)(2,1)S(1)} fusion(bf16[1536,384]{1,0:T(8,128)(2,1)S(1)} %slice.88, bf16[256,384]{1,0:T(8,128)(2,1)S(1)} %bitcast.93, bf16[256,384]{1,0:T(8,128)(2,1)S(1)} %bitcast.90, bf16[1024,384]{1,0:T(8,128)(2,1)S(1)} %bitcast.78, bf16[1024,384]{1,0:T(8,128)(2,1)S(1)} %collective-permute-done.4, ...), kind=kOutput, calls=%fused_computation.5 | convolution fusion | flops 2430074880 | bytes 7077888 | tf_op jit(solution)/shard_map/dot_general | solution.py:251
  270.3 2.7 pad_maximum_fusion
  274.1 4.1 %fusion.11 = bf16[384,2048]{1,0:T(8,128)(2,1)S(1)} fusion(bf16[1024,384]{1,0:T(8,128)(2,1)S(1)} %bitcast.75, bf16[2048,2560]{1,0:T(8,128)(2,1)} %all-gather.2.cloned.1.call-done), kind=kOutput, calls=%fused_computation.17 | convolution fusion | flops 1611399168 | bytes 6553600 | tf_op jit(solution)/shard_map/dot_general | solution.py:269
  278.7 80.7 %reduce-scatter.2.cloned.1.call-done = bf16[64,2560]{1,0:T(8,128)(2,1)} async-done(((bf16[1024,2560]{1,0:T(8,128)(2,1)}), bf16[64,2560]{1,0:T(8,128)(2,1)}) %reduce-scatter.2.cloned.1.call-update) | async-done | bytes 327696 | tf_op jit(solution)/shard_map/reduce_scatter | solution.py:265
  359.4 4.2 %all-to-all-start.2 = ((bf16[4,16,2560]{2,1,0:T(8,128)(2,1)}), bf16[4,16,2560]{2,1,0:T(8,128)(2,1)S(1)}, u32[]{:S(2)}, u32[]{:S(2)}) async-start(bf16[4,16,2560]{2,1,0:T(8,128)(2,1)} %bitcast.94), calls=%async_computation.3 | async-start | bytes 655360 | tf_op jit(solution)/shard_map/all_to_all | solution.py:266
  365.2 2.3 collective-permute-done
  367.5 2.7 collective-permute-start.1
  370.2 2.4 collective-permute-done.1
  373.9 2.3 collective-permute-done.2
  376.2 2.6 collective-permute-start.3
  378.8 2.5 collective-permute-done.3
  (75 shorter events, 13.2 us)
Async XLA Ops:
  7.2 78.7 %all-gather.2.cloned.1.call-start = ((), (), s32[]{:S(2)}) async-start(), calls=%async_computation.4 | async-start | bytes 10567680 | tf_op jit(solution)/shard_map/all_gather | solution.py:183
  92.5 1.4 copy-start.9
  100.7 54.0 %copy-start.1 = (s32[3,8]{1,0:T(4,128)S(1)}, s32[3,8]{1,0:T(4,128)}, u32[]{:S(2)}) copy-start(s32[3,8]{1,0:T(4,128)} %ends_ref.1) | copy-start | bytes 292
  100.7 54.0 %all-to-all-start = ((bf16[16,256,384]{2,1,0:T(8,128)(2,1)}), bf16[16,256,384]{2,1,0:T(8,128)(2,1)S(1)}, u32[]{:S(2)}, u32[]{:S(2)}) async-start(bf16[16,256,384]{2,1,0:T(8,128)(2,1)} %pad_maximum_fusion.1), calls=%async_computation | async-start | bytes 6291456 | tf_op jit(solution)/shard_map/all_to_all | solution.py:227
  154.7 1.0 copy-start
  197.8 42.8 %all-to-all-start.1 = ((bf16[16,256,384]{2,1,0:T(8,128)(2,1)}), bf16[16,256,384]{2,1,0:T(8,128)(2,1)S(1)}, u32[]{:S(2)}, u32[]{:S(2)}) async-start(bf16[16,256,384]{2,1,0:T(8,128)(2,1)} %attention.1), calls=%async_computation.1 | async-start | bytes 6291456 | tf_op jit(solution)/shard_map/all_to_all | solution.py:233
  202.2 157.1 %reduce-scatter.2.cloned.1.call-start = ((), (), s32[]{:S(2)}) async-start(), calls=%async_computation.5 | async-start | bytes 5570560 | tf_op jit(solution)/shard_map/reduce_scatter | solution.py:265
  207.6 52.6 %collective-permute-start.6 = (bf16[1024,384]{1,0:T(8,128)(2,1)}, bf16[1024,384]{1,0:T(8,128)(2,1)}, u32[]{:S(2)}, u32[]{:S(2)}) collective-permute-start(bf16[1024,384]{1,0:T(8,128)(2,1)} %bitcast.26), channel_id=1, source_target_pairs={{0,1},{1,0},{2,3},{3,2},{4,5},{5,4},{6,7},{7,6},{8,9},{9,8},{10,11... | collective-permute-start | bytes 2359304 | tf_op jit(solution)/shard_map/ppermute | solution.py:200
  240.6 1.6 copy-start.3
  242.4 3.9 %copy-start.4 = (bf16[16,64,384]{2,1,0:T(8,128)(2,1)}, bf16[16,64,384]{2,1,0:T(8,128)(2,1)S(1)}, u32[]{:S(2)}) copy-start(bf16[16,64,384]{2,1,0:T(8,128)(2,1)S(1)} %get-tuple-element.10) | copy-start | bytes 2359300
  242.4 10.0 %copy-start.7 = (bf16[16,64,384]{2,1,0:T(8,128)(2,1)}, bf16[16,64,384]{2,1,0:T(8,128)(2,1)S(1)}, u32[]{:S(2)}) copy-start(bf16[16,64,384]{2,1,0:T(8,128)(2,1)S(1)} %get-tuple-element.9) | copy-start | bytes 2359300
  242.4 3.9 copy-start.2
  242.4 3.9 copy-start.13
  246.3 11.3 %collective-permute-start.5 = (bf16[2560,384]{1,0:T(8,128)(2,1)}, bf16[2560,384]{1,0:T(8,128)(2,1)}, u32[]{:S(2)}, u32[]{:S(2)}) collective-permute-start(bf16[2560,384]{1,0:T(8,128)(2,1)} %pad_maximum_fusion.2), channel_id=1, source_target_pairs={{0,1},{1,0},{2,3},{3,2},{4,5},{5,4},{6,7},{7,6},{8,9},{9,8},{10,11... | collective-permute-start | bytes 5898248 | tf_op jit(solution)/shard_map/ppermute | solution.py:246
  256.8 3.4 copy-start.5
  256.8 3.4 copy-start.11
  257.0 6.3 %collective-permute-start.4 = (bf16[1024,384]{1,0:T(8,128)(2,1)S(1)}, bf16[1024,384]{1,0:T(8,128)(2,1)S(1)}, u32[]{:S(2)}, u32[]{:S(2)}) collective-permute-start(bf16[1024,384]{1,0:T(8,128)(2,1)S(1)} %bitcast.86), channel_id=1, source_target_pairs={{0,1},{1,0},{2,3},{3,2},{4,5},{5,4},{6,7},{7,6},{8,9},{9,8},{10,11... | collective-permute-start | bytes 2359304 | tf_op jit(solution)/shard_map/ppermute | solution.py:200
  260.2 3.1 copy-start.8
  273.0 1.1 copy-start.6
  274.1 89.5 %copy-start.12 = (f32[2048]{0:T(1024)S(1)}, f32[2048]{0:T(1024)}, u32[]{:S(2)}) copy-start(f32[2048]{0:T(1024)} %param.17) | copy-start | bytes 24580
  278.2 104.9 %copy-start.10 = (bf16[384,2048]{1,0:T(8,128)(2,1)}, bf16[384,2048]{1,0:T(8,128)(2,1)S(1)}, u32[]{:S(2)}) copy-start(bf16[384,2048]{1,0:T(8,128)(2,1)S(1)} %fusion.11) | copy-start | bytes 4718596
  359.4 22.5 %all-to-all-start.2 = ((bf16[4,16,2560]{2,1,0:T(8,128)(2,1)}), bf16[4,16,2560]{2,1,0:T(8,128)(2,1)S(1)}, u32[]{:S(2)}, u32[]{:S(2)}) async-start(bf16[4,16,2560]{2,1,0:T(8,128)(2,1)} %bitcast.94), calls=%async_computation.3 | async-start | bytes 655360 | tf_op jit(solution)/shard_map/all_to_all | solution.py:266
  363.9 3.6 collective-permute-start
  367.5 5.1 %collective-permute-start.1 = (f32[3,8]{1,0:T(4,128)S(1)}, f32[3,8]{1,0:T(4,128)S(1)}, u32[]{:S(2)}, u32[]{:S(2)}) collective-permute-start(f32[3,8]{1,0:T(4,128)S(1)} %add.74), channel_id=1, source_target_pairs={{0,16},{8,24},{16,0},{24,8},{32,48},{40,56},{48,32},{56,40},{64,80... | collective-permute-start | bytes 296 | tf_op jit(solution)/shard_map/ppermute | solution.py:285
  372.6 3.6 collective-permute-start.2
  376.2 5.1 %collective-permute-start.3 = (f32[3,8]{1,0:T(4,128)S(1)}, f32[3,8]{1,0:T(4,128)S(1)}, u32[]{:S(2)}, u32[]{:S(2)}) collective-permute-start(f32[3,8]{1,0:T(4,128)S(1)} %add.76), channel_id=1, source_target_pairs={{0,64},{8,72},{16,80},{24,88},{32,96},{40,104},{48,112},{56,120},{... | collective-permute-start | bytes 296 | tf_op jit(solution)/shard_map/ppermute | solution.py:285
Sparse Core Ops, SparseCore 0:
  11.7 74.0 all-gather.1
  273.1 86.1 reduce-scatter.1

commit v2 on v1

v2 whole, which is shorter than its diff:
```python
import jax
import jax.numpy as jnp
from jax import lax
from jax.experimental import pallas as pl
from jax.experimental.pallas import tpu as pltpu
from jax.sharding import Mesh
from jax.sharding import PartitionSpec as P

HEADS = 16
KV_HEADS = 4
HEAD_DIM = 64
GROUP = HEADS // KV_HEADS
HALF = HEAD_DIM // 2
BLOCK = 256

eps = 1e-05
base_theta = 500000.0


def rotation_tables(positions):
    freqs = base_theta ** (-(2.0 * jnp.arange(HALF, dtype=jnp.float32)) / HEAD_DIM)
    angles = positions.astype(jnp.float32)[None, :] * freqs[:, None]
    return jnp.cos(angles), jnp.sin(angles)


def pair_lists(end_rows, blocks):
    at = jnp.arange(blocks, dtype=jnp.int32) * BLOCK
    after = end_rows[:, None, :] + 1
    first = jnp.max(jnp.where(after <= at[None, :, None], after, 0), -1) // BLOCK
    codes = [(i, i - d) for d in range(1, blocks) for i in range(d, blocks)]
    query = jnp.array([i for i, _ in codes], jnp.int32)
    key = jnp.array([j for _, j in codes], jnp.int32)
    lowest = jnp.stack([first[:, i] for i, _ in codes], 1)
    valid = key[None] >= lowest
    place = jnp.cumsum(valid.astype(jnp.int32), 1) - 1
    slot = jnp.arange(len(codes), dtype=jnp.int32)
    chosen = valid[:, :, None] & (place[:, :, None] == slot)
    listed = jnp.sum(jnp.where(chosen, (query * blocks + key)[None, :, None], 0), 1)
    counts = jnp.sum(valid.astype(jnp.int32), 1)
    listed = jnp.where(slot[None] < counts[:, None], listed, blocks - 1)
    return listed, jnp.max(counts).reshape(1)


def block_of(ref, part, slab, b, rows):
    per = BLOCK // rows
    return jnp.concatenate(
        [
            ref[
                b * per + r,
                part * HEAD_DIM : (part + 1) * HEAD_DIM,
                slab * rows : (slab + 1) * rows,
            ]
            for r in range(per)
        ],
        axis=1,
    )


def mask_of(starts, i, j):
    place = lax.broadcasted_iota(jnp.int32, (1, BLOCK), 1) + i * BLOCK
    key = lax.broadcasted_iota(jnp.int32, (BLOCK, BLOCK), 0) + j * BLOCK
    return (key >= starts) & (key <= place)


def starts_of(ends_ref, slab, b):
    place = lax.broadcasted_iota(jnp.int32, (1, BLOCK), 1) + b * BLOCK
    start = jnp.zeros((1, BLOCK), jnp.int32)
    for d in range(ends_ref.shape[1] - 1):
        after = ends_ref[slab, d] + 1
        start = jnp.where(place >= after, after, start)
    return start


def forward_kernel(
    ends_ref, pairs_ref, count_ref, in_ref, out_ref, stats_ref, q_s, k_s, vt_s, start_s, top_s, sum_s, acc_s
):
    slabs = ends_ref.shape[0]
    n_src = in_ref.shape[0]
    rows = in_ref.shape[2] // slabs
    per = BLOCK // rows
    blocks = n_src // per
    f32, bf16 = jnp.float32, jnp.bfloat16

    for s in range(slabs):
        for b in range(blocks):
            at = s * blocks + b
            q_s[at] = block_of(in_ref, 0, s, b, rows)
            k_s[at] = block_of(in_ref, 1, s, b, rows).T
            vt_s[at] = block_of(in_ref, 2, s, b, rows)
            start_s[at] = starts_of(ends_ref, s, b)

    def scores(s, i, j):
        raw = jnp.dot(k_s[s * blocks + j], q_s[s * blocks + i], preferred_element_type=f32)
        return jnp.where(mask_of(start_s[s * blocks + i], i, j), raw, -jnp.inf)

    def weighted(w, at):
        over_keys = (((0,), (1,)), ((), ()))
        return lax.dot_general(
            w.astype(bf16), vt_s[at], over_keys, preferred_element_type=f32
        ).T

    def diagonal(i, _):
        done = []
        for s in range(slabs):
            raw = scores(s, i, i)
            top = jnp.max(raw, axis=0, keepdims=True)
            w = jnp.exp(raw - top)
            total = jnp.sum(w, axis=0, keepdims=True)
            acc = weighted(w, s * blocks + i)
            done.append((top, total, acc))
        for s in range(slabs):
            at = s * blocks + i
            top_s[at], sum_s[at], acc_s[at] = done[s]
        return 0

    lax.fori_loop(0, blocks, diagonal, 0, unroll=True)

    def below(step, _):
        done = []
        for s in range(slabs):
            code = pairs_ref[s, step]
            i, j = lax.div(code, blocks), lax.rem(code, blocks)
            at = s * blocks + i
            raw = scores(s, i, j)
            old = top_s[at]
            top = jnp.maximum(old, jnp.max(raw, axis=0, keepdims=True))
            fade = jnp.exp(old - top)
            w = jnp.exp(raw - top)
            total = sum_s[at] * fade + jnp.sum(w, axis=0, keepdims=True)
            acc = acc_s[at] * fade + weighted(w, s * blocks + j)
            done.append((at, top, total, acc))
        for at, top, total, acc in done:
            top_s[at], sum_s[at], acc_s[at] = top, total, acc
        return 0

    lax.fori_loop(0, count_ref[0], below, 0)

    for s in range(slabs):
        for b in range(blocks):
            at = s * blocks + b
            inv = 1.0 / sum_s[at]
            stats_ref[at, 0:1, :] = top_s[at]
            stats_ref[at, 1:2, :] = inv
            ctx = (acc_s[at] * inv).astype(bf16)
            for r in range(per):
                out_ref[b * per + r, :, s * rows : (s + 1) * rows] = ctx[
                    :, r * rows : (r + 1) * rows
                ]


def backward_kernel(
    ends_ref,
    pairs_ref,
    count_ref,
    in_ref,
    grad_ref,
    ctx_ref,
    stats_ref,
    cos_ref,
    sin_ref,
    out_ref,
    q_s,
    kt_s,
    k_s,
    v_s,
    g_s,
    start_s,
    delta_s,
    dq_s,
    dk_s,
    dv_s,
):
    slabs = ends_ref.shape[0]
    n_src = in_ref.shape[0]
    rows = in_ref.shape[2] // slabs
    per = BLOCK // rows
    blocks = n_src // per
    f32, bf16 = jnp.float32, jnp.bfloat16
    hd = HEAD_DIM

    for s in range(slabs):
        for b in range(blocks):
            at = s * blocks + b
            kt = block_of(in_ref, 1, s, b, rows)
            grad = block_of(grad_ref, 0, s, b, rows)
            ctx = block_of(ctx_ref, 0, s, b, rows)
            q_s[at] = block_of(in_ref, 0, s, b, rows)
            kt_s[at] = kt
            k_s[at] = kt.T
            v_s[at] = block_of(in_ref, 2, s, b, rows).T
            g_s[at] = grad
            start_s[at] = starts_of(ends_ref, s, b)
            delta_s[at] = jnp.sum(grad.astype(f32) * ctx.astype(f32), axis=0, keepdims=True)

    trans = (((1,), (1,)), ((), ()))

    def terms(s, i, j):
        qi, kj = s * blocks + i, s * blocks + j
        query, grad = q_s[qi], g_s[qi]
        raw = jnp.dot(k_s[kj], query, preferred_element_type=f32)
        raw = jnp.where(mask_of(start_s[qi], i, j), raw, -jnp.inf)
        probs = jnp.exp(raw - stats_ref[qi, 0:1, :]) * stats_ref[qi, 1:2, :]
        dp = jnp.dot(v_s[kj], grad, preferred_element_type=f32)
        ds = (probs * (dp - delta_s[qi])).astype(bf16)
        dv = lax.dot_general(grad, probs.astype(bf16), trans, preferred_element_type=f32)
        dk = lax.dot_general(query, ds, trans, preferred_element_type=f32)
        dq = jnp.dot(kt_s[kj], ds, preferred_element_type=f32)
        return qi, kj, dq, dk, dv

    def diagonal(i, _):
        done = [terms(s, i, i) for s in range(slabs)]
        for qi, kj, dq, dk, dv in done:
            dq_s[qi], dk_s[kj], dv_s[kj] = dq, dk, dv
        return 0

    lax.fori_loop(0, blocks, diagonal, 0, unroll=True)

    def below(step, _):
        done = []
        for s in range(slabs):
            code = pairs_ref[s, step]
            qi, kj, dq, dk, dv = terms(s, lax.div(code, blocks), lax.rem(code, blocks))
            done.append((qi, kj, dq_s[qi] + dq, dk_s[kj] + dk, dv_s[kj] + dv))
        for qi, kj, dq, dk, dv in done:
            dq_s[qi], dk_s[kj], dv_s[kj] = dq, dk, dv
        return 0

    lax.fori_loop(0, count_ref[0], below, 0)

    for s in range(slabs):
        for b in range(blocks):
            at = s * blocks + b
            for r in range(per):
                lanes = slice(r * rows, (r + 1) * rows)
                src, here = b * per + r, slice(s * rows, (s + 1) * rows)
                cosine, sine = cos_ref[src], sin_ref[src]
                for n, grads, factor in ((0, dq_s, hd**-0.5), (1, dk_s, None)):
                    x, y = grads[at, :HALF, lanes], grads[at, HALF:, lanes]
                    if factor is not None:
                        x, y = x * factor, y * factor
                    out_ref[src, n * hd : n * hd + HALF, here] = (
                        x * cosine + y * sine
                    ).astype(bf16)
                    out_ref[src, n * hd + HALF : (n + 1) * hd, here] = (
                        y * cosine - x * sine
                    ).astype(bf16)
                out_ref[src, 2 * hd : 3 * hd, here] = dv_s[at, :, lanes].astype(bf16)


SMEM = pl.BlockSpec(memory_space=pltpu.SMEM)
VMEM = pl.BlockSpec(memory_space=pltpu.VMEM)
VMEM_LIMIT = 48 * 1024 * 1024


def attend(received, ends, pairs, count):
    n_src, _, tok = received.shape
    n = n_src * tok // BLOCK
    bf16, f32 = jnp.bfloat16, jnp.float32
    wide = pltpu.VMEM((n, HEAD_DIM, BLOCK), bf16)
    row = pltpu.VMEM((n, 1, BLOCK), f32)
    return pl.pallas_call(
        forward_kernel,
        out_shape=(
            jax.ShapeDtypeStruct((n_src, HEAD_DIM, tok), bf16),
            jax.ShapeDtypeStruct((n, 2, BLOCK), f32),
        ),
        in_specs=[SMEM, SMEM, SMEM, VMEM],
        out_specs=(VMEM, VMEM),
        scratch_shapes=[
            wide,
            pltpu.VMEM((n, BLOCK, HEAD_DIM), bf16),
            wide,
            pltpu.VMEM((n, 1, BLOCK), jnp.int32),
            row,
            row,
            pltpu.VMEM((n, HEAD_DIM, BLOCK), f32),
        ],
        compiler_params=pltpu.CompilerParams(vmem_limit_bytes=VMEM_LIMIT),
        cost_estimate=pl.CostEstimate(
            flops=8 * 10**9, bytes_accessed=4 * 2**20, transcendentals=3 * 2**20
        ),
        name="attend",
    )(ends, pairs, count, received)


def attend_back(received, grads, context, stats, ends, pairs, count, cos_all, sin_all):
    n_src, _, tok = received.shape
    n = n_src * tok // BLOCK
    bf16, f32 = jnp.bfloat16, jnp.float32
    wide = pltpu.VMEM((n, HEAD_DIM, BLOCK), bf16)
    tall = pltpu.VMEM((n, BLOCK, HEAD_DIM), bf16)
    total = pltpu.VMEM((n, HEAD_DIM, BLOCK), f32)
    return pl.pallas_call(
        backward_kernel,
        out_shape=jax.ShapeDtypeStruct(received.shape, bf16),
        in_specs=[SMEM, SMEM, SMEM] + [VMEM] * 6,
        out_specs=VMEM,
        scratch_shapes=[
            wide,
            wide,
            tall,
            tall,
            wide,
            pltpu.VMEM((n, 1, BLOCK), jnp.int32),
            pltpu.VMEM((n, 1, BLOCK), f32),
            total,
            total,
            total,
        ],
        compiler_params=pltpu.CompilerParams(vmem_limit_bytes=VMEM_LIMIT),
        cost_estimate=pl.CostEstimate(
            flops=16 * 10**9, bytes_accessed=8 * 2**20, transcendentals=3 * 2**20
        ),
        name="attend_back",
    )(ends, pairs, count, received, grads, context, stats, cos_all, sin_all)


def on_device(
    tokens,
    segment_ids,
    end_rows,
    input_norm_gain,
    query_weight,
    key_weight,
    value_weight,
    out_weight,
    head_weight,
    branch_grad,
):
    del segment_ids
    bf16, f32 = jnp.bfloat16, jnp.float32
    n_ctx, n_x, n_core = (lax.axis_size(a) for a in ("ctx", "x", "core"))
    rank = lax.axis_index("ctx")
    core = lax.axis_index("core")
    slabs, rows, model = tokens.shape
    docs = end_rows.shape[1]
    tok = slabs * rows
    width = HEADS * HEAD_DIM
    kv_width = KV_HEADS * HEAD_DIM
    qkv = width + 2 * kv_width
    swap = [(c, n_core - 1 - c) for c in range(n_core)]

    weights = lax.all_gather(
        jnp.concatenate([query_weight, key_weight, value_weight, out_weight], 1),
        ("ctx", "x", "core"),
        axis=0,
        tiled=True,
    )

    flat = tokens.reshape(tok, model)
    grad_out = branch_grad.reshape(tok, model)
    wide = flat.astype(f32)
    inverse_norm = lax.rsqrt(jnp.mean(wide * wide, -1, keepdims=True) + eps)
    normed = (wide * inverse_norm * input_norm_gain).astype(bf16)

    def by_core(values):
        split = values.T.reshape(model // (16 * n_core), n_core, 16, tok)
        mine = lax.dynamic_index_in_dim(split, core, 1, keepdims=False).reshape(-1, tok)
        other = lax.dynamic_index_in_dim(split, 1 - core, 1, keepdims=False).reshape(-1, tok)
        return mine, lax.ppermute(other, "core", swap)

    normed_mine, normed_other = by_core(normed)
    grad_out_mine, grad_out_other = by_core(grad_out)

    first = rank * rows
    cos_all, sin_all = rotation_tables(jnp.arange(n_ctx * rows, dtype=jnp.int32))
    cos_here, sin_here = rotation_tables(first + jnp.arange(rows, dtype=jnp.int32))
    cos_here = jnp.tile(cos_here, (1, slabs))[None]
    sin_here = jnp.tile(sin_here, (1, slabs))[None]
    over = (((0,), (1,)), ((), ()))
    projected = lax.dot_general(weights[:, :qkv], normed, over, preferred_element_type=f32)
    turning = projected[: width + kv_width].reshape(HEADS + KV_HEADS, 2, HALF, tok)
    front, back = turning[:, 0], turning[:, 1]
    turned = jnp.concatenate(
        [front * cos_here - back * sin_here, back * cos_here + front * sin_here], 1
    )
    query = (turned[:HEADS] * (HEAD_DIM**-0.5)).astype(bf16)
    keys = jnp.repeat(turned[HEADS:].astype(bf16), GROUP, axis=0)
    values = projected[width + kv_width :].astype(bf16).reshape(KV_HEADS, HEAD_DIM, tok)
    values = jnp.repeat(values, GROUP, axis=0)
    send = jnp.concatenate([query, keys, values], 1)
    received = lax.all_to_all(send, "ctx", split_axis=0, concat_axis=0, tiled=True)
    context_grad = lax.dot_general(
        weights[:, qkv:], grad_out, over, preferred_element_type=f32
    ).astype(bf16)
    grads_in = lax.all_to_all(
        context_grad.reshape(HEADS, HEAD_DIM, tok), "ctx", split_axis=0, concat_axis=0, tiled=True
    )

    pairs, count = pair_lists(end_rows, n_ctx * rows // BLOCK)
    context_head, stats = attend(received, end_rows, pairs, count)
    context_head, grads_in = lax.optimization_barrier((context_head, grads_in))
    context = lax.all_to_all(context_head, "ctx", split_axis=0, concat_axis=0, tiled=True)

    def by_source(table):
        return jnp.swapaxes(table.reshape(HALF, n_ctx, rows), 0, 1)

    results = attend_back(
        received,
        grads_in,
        context_head,
        stats,
        end_rows,
        pairs,
        count,
        by_source(cos_all),
        by_source(sin_all),
    )
    back_home = lax.all_to_all(results, "ctx", split_axis=0, concat_axis=0, tiled=True)
    last = (((1,), (1,)), ((), ()))

    def both_cores(a, b, c, d):
        return lax.dot_general(
            jnp.concatenate([a, c], 1),
            jnp.concatenate([b, d], 1),
            last,
            preferred_element_type=f32,
        ).astype(bf16)

    context = context.reshape(width, tok)
    context_other = lax.ppermute(context, "core", swap)
    partial_out = both_cores(grad_out_mine, context, grad_out_other, context_other)

    branch = lax.dot_general(context, weights[:, qkv:], over, preferred_element_type=f32)
    branch = branch.astype(bf16)
    here = jnp.arange(slabs, dtype=jnp.int32)
    marks = (
        (end_rows[:, :, None, None] == first + jnp.arange(rows, dtype=jnp.int32))
        & (here[:, None, None, None] == here[:, None])
    ).astype(bf16)
    marks = marks.reshape(slabs * docs, tok)
    picked = jnp.dot(marks, flat, preferred_element_type=f32) + jnp.dot(
        marks, branch, preferred_element_type=f32
    )
    picked = picked * lax.rsqrt(jnp.mean(picked * picked, -1, keepdims=True) + eps)
    rewards = jnp.sum(picked * head_weight, -1).reshape(slabs, docs)
    hd = HEAD_DIM
    back_home, partial_out = lax.optimization_barrier((back_home, partial_out))
    pieces_out = lax.all_to_all(
        partial_out, ("ctx", "x"), split_axis=0, concat_axis=0, tiled=True
    )
    dquery = back_home[:, :hd].reshape(width, tok)

    def over_group(heads):
        heads = heads.astype(f32).reshape(KV_HEADS, GROUP, hd, tok)
        return jnp.sum(heads, 1).astype(bf16).reshape(kv_width, tok)

    dkey = over_group(back_home[:, hd : 2 * hd])
    dvalue = over_group(back_home[:, 2 * hd :])
    grads = jnp.concatenate([dquery, dkey, dvalue], 0)
    grads_other = lax.ppermute(grads, "core", swap)
    partial = both_cores(normed_mine, grads, normed_other, grads_other)
    partial, grads, context = lax.optimization_barrier((partial, grads, context))
    chunks, parts = n_ctx * n_x, []
    rest = rewards.reshape(-1)
    for _ in range(3):
        part = lax.reduce_precision(rest, 8, 7)
        parts.append(part)
        rest = rest - part
    riders = jnp.stack(parts, 0).astype(bf16)
    extra = 128
    riders = jnp.pad(riders, ((0, 16 - len(parts)), (0, extra - riders.shape[1])))
    partial = jnp.concatenate([partial, jnp.tile(riders, (chunks, 1))], 1)
    pieces = lax.all_to_all(partial, ("ctx", "x"), split_axis=0, concat_axis=0, tiled=True)
    dnormed = lax.dot_general(grads, weights[:, :qkv], over, preferred_element_type=f32)
    scaled = dnormed * input_norm_gain
    centered = wide * inverse_norm
    grad_tokens = inverse_norm * (
        scaled - centered * jnp.mean(scaled * centered, -1, keepdims=True)
    )
    pieces = pieces.reshape(chunks, -1, qkv + extra)
    summed = jnp.sum(pieces[:, :, :qkv].astype(f32), 0)
    summed_out = jnp.sum(pieces_out.reshape(chunks, -1, width).astype(f32), 0)
    riders = pieces[:, : len(parts), qkv:].reshape(n_ctx, n_x, len(parts), extra)
    riders = lax.dynamic_index_in_dim(riders, lax.axis_index("x"), 1, keepdims=False)
    rewards = jnp.sum(riders[:, :, : slabs * docs].astype(f32), (0, 1)).reshape(slabs, docs)
    return (
        branch.reshape(tokens.shape),
        rewards,
        grad_tokens.astype(bf16).reshape(tokens.shape),
        summed[:, :width],
        summed[:, width : width + kv_width],
        summed[:, width + kv_width :],
        summed_out,
    )


def solution(mesh):
    n_ctx, n_fsdp = mesh.devices.shape
    chips = Mesh(mesh.devices.reshape(n_ctx, n_fsdp // 2, 2), ("ctx", "x", "core"))
    fsdp = ("x", "core")
    rows = P(("ctx", "x", "core"), None)
    acts = P(fsdp, "ctx", None)
    return jax.shard_map(
        on_device,
        mesh=chips,
        in_specs=(
            acts,
            P(fsdp, None),
            P(fsdp, None),
            P(),
            rows,
            rows,
            rows,
            rows,
            P(),
            acts,
        ),
        out_specs=(acts, P(fsdp, None), acts, rows, rows, rows, rows),
        check_vma=False,
    )
```

time: 391 us -> 335 us (0.86)
  waiting for transfers between devices: 245 us -> 160 us
  starting transfers between devices: 22.5 us -> 41.6 us
  other arithmetic: 17.6 us -> 22.1 us
    reduce_scatter x1 -> x0, waiting for transfers between devices: 80.7 us -> none  [on_device(): summed = lax.psum_scatter(partial, 'ctx', scatter_dimension=0, tiled=True)]
    all_to_all x1 -> x4, waiting for transfers between devices: 0.01 us -> 47.6 us  [the longest x1 34.6 us: on_device(): lax.all_to_all(partial, ('ctx', 'x'), split_axis=0, concat_axis=0, tiled=...]
    all_to_all x1, waiting for transfers between devices: 33 us -> 7.37 us  [on_device(): lax.all_to_all(results, 'ctx', split_axis=0, concat_axis=0, tiled=True)]
    all_to_all x1 -> x4, starting transfers between devices: 4.22 us -> 28.3 us  [the longest x1 11.3 us: on_device(): lax.all_to_all(partial_out, ('ctx', 'x'), split_axis=0, concat_axis=0, ti...]
    all_to_all x1, waiting for transfers between devices: 46.9 us -> 27.5 us  [on_device(): lax.all_to_all(send, 'ctx', split_axis=0, concat_axis=0, tiled=True)]
    ppermute x5 -> x2, starting transfers between devices: 7.87 us -> 0.59 us  [the longest x1 0.51 us: on_device(): context_other = lax.ppermute(context, 'core', swap)]
    ppermute x5 -> x2, waiting for transfers between devices: 9.49 us -> 2.25 us  [the longest x1 2.25 us: on_device(): context_other = lax.ppermute(context, 'core', swap)]
    reduce_sum x1 -> x5, other arithmetic: 0.04 us -> 5.19 us  [the longest x1 2.58 us: on_device(): summed_out = jnp.sum(pieces_out.reshape(chunks, -1, width).astype(f32), 0)]
  transfers between devices with their start and end apart: 12 -> 11, of which waited for: 8 -> 7; matrix products, arithmetic and copies ran while one was open for 9% -> 16% of each run, Pallas kernels for 0% -> 14%
where the time goes in v2:
time: 335 us
  waiting for transfers between devices  160 us (48%)
  Pallas kernels  45.9 us (14%)
  starting transfers between devices  41.6 us (12%)
  matrix products  34.2 us (10%)
  other arithmetic  22.1 us (7%)
  local copies, waits for them, and re-layouts  16.7 us (5%)
  between operations  14.5 us (4%)
    all_gather x1, waiting for transfers between devices, on_device(): lax.all_gather(jnp.concatenate([query_weight, key_weight, value_weight, o...  75.1 us
    all_to_all x1, waiting for transfers between devices, on_device(): lax.all_to_all(partial, ('ctx', 'x'), split_axis=0, concat_axis=0, tiled=...  34.6 us
    all_to_all x1, waiting for transfers between devices, on_device(): lax.all_to_all(send, 'ctx', split_axis=0, concat_axis=0, tiled=True)  27.5 us
    pallas_call x1, Pallas kernels, attend_back(): pl.pallas_call(backward_kernel, out_shape=jax.ShapeDtypeStruct(received.s...  27.3 us
    pallas_call x1, Pallas kernels, attend(): pl.pallas_call(forward_kernel, out_shape=(jax.ShapeDtypeStruct((n_src, HE...  18.6 us
    all_to_all x1, waiting for transfers between devices, on_device(): lax.all_to_all(partial_out, ('ctx', 'x'), split_axis=0, concat_axis=0, ti...  13 us
    all_to_all x1, starting transfers between devices, on_device(): lax.all_to_all(partial_out, ('ctx', 'x'), split_axis=0, concat_axis=0, ti...  11.3 us
    dot_general x2, matrix products, both_cores(): lax.dot_general(jnp.concatenate([a, c], 1), jnp.concatenate([b, d], 1), l...  11.2 us
  transfers between devices with their start and end apart: 11, of which 7 were waited for; matrix products, arithmetic and copies ran while one was open for 16% of the time, Pallas kernels for 14%

profile of v2, /device:TPU:0, one launch (start us, length us, event | category | flops | bytes accessed | tf_op | source)
XLA Modules:
  0.0 335.4 jit_solution(6233982245383381474)
XLA Ops:
  7.2 1.5 pad_maximum_fusion.4
  8.7 1.8 multiply_reduce_fusion.1
  10.7 75.1 %all-gather.2.cloned.1.call-done = bf16[2048,2560]{1,0:T(8,128)(2,1)} async-done(((bf16[16,2560]{1,0:T(8,128)(2,1)}), bf16[2048,2560]{1,0:T(8,128)(2,1)}) %all-gather.2.cloned.1.call-update) | async-done | bytes 10485776 | tf_op jit(solution)/shard_map/all_gather | solution.py:343
  85.8 6.2 %fusion.2 = f32[1536,384]{1,0:T(8,128)S(1)} fusion(bf16[2048,2560]{1,0:T(8,128)(2,1)} %all-gather.2.cloned.1.call-done, bf16[384,2048]{1,0:T(8,128)(2,1)} %bitcast.79, f32[2048]{0:T(1024)} %param.14, f32[384]{0:T(512)S(1)} %rsqrt_bitcast_fusion), kind=kOutput, calls=%fused_computation.3 | convolution fusion | flops 2419064832 | bytes 10233344 | tf_op jit(solution)/shard_map/dot_general | solution.py:371
  92.9 1.7 pad_maximum_fusion.1
  94.6 5.3 %all-to-all-start = ((bf16[16,192,384]{2,1,0:T(8,128)(2,1)}), bf16[16,192,384]{2,1,0:T(8,128)(2,1)S(1)}, u32[]{:S(2)}, u32[]{:S(2)}) async-start(bf16[16,192,384]{2,1,0:T(8,128)(2,1)} %pad_maximum_fusion.1), calls=%async_computation | async-start | bytes 4718592 | tf_op jit(solution)/shard_map/all_to_all | solution.py:382
  102.0 1.7 multiply_sine_fusion
  103.7 5.9 %fusion.33 = bf16[1024,384]{1,0:T(8,128)(2,1)} fusion(bf16[384,2048]{1,0:T(8,128)(2,1)} %bitcast.90, bf16[2048,2560]{1,0:T(8,128)(2,1)} %all-gather.2.cloned.1.call-done), kind=kOutput, calls=%fused_computation.43 | convolution fusion | flops 1611005952 | bytes 6553600 | tf_op jit(solution)/shard_map/dot_general | solution.py:383
  109.7 27.5 %all-to-all-done.in_ref = bf16[16,192,384]{2,1,0:T(8,128)(2,1)S(1)} async-done(((bf16[16,192,384]{2,1,0:T(8,128)(2,1)}), bf16[16,192,384]{2,1,0:T(8,128)(2,1)S(1)}, u32[]{:S(2)}, u32[]{:S(2)}) %all-to-all-start) | async-done | bytes 2359328 | tf_op jit(solution)/shard_map/all_to_all | solution.py:382
  137.1 3.9 %all-to-all-start.1 = ((bf16[16,64,384]{2,1,0:T(8,128)(2,1)}), bf16[16,64,384]{2,1,0:T(8,128)(2,1)S(1)}, u32[]{:S(2)}, u32[]{:S(2)}) async-start(bf16[16,64,384]{2,1,0:T(8,128)(2,1)} %bitcast.97), calls=%async_computation.1 | async-start | bytes 1572864 | tf_op jit(solution)/shard_map/all_to_all | solution.py:386
  141.0 18.6 %attend.1 = (bf16[16,64,384]{2,1,0:T(8,128)(2,1)S(1)}, f32[24,2,256]{2,1,0:T(2,128)S(1)}) custom-call(s32[3,8]{1,0:T(4,128)S(1)} %copy-done.4, s32[3,28]{1,0:T(4,128)S(1)} %fusion.58.pairs_ref, s32[1]{0:T(128)} %bitcast.count_ref, bf16[16,192,384]{2,1,0:T(8,128)(2,1)S(1)} %all-to-all-done.in_ref), custom_call_target="tpu_custom_call" | custom-call | flops 8000000000 | bytes 4194304 | tf_op jit(solution)/shard_map/attend/pallas_call | solution.py:261
  160.6 7.2 %all-to-all-start.2 = ((bf16[16,64,384]{2,1,0:T(8,128)(2,1)}), bf16[16,64,384]{2,1,0:T(8,128)(2,1)S(1)}, u32[]{:S(2)}, u32[]{:S(2)}) async-start(bf16[16,64,384]{2,1,0:T(8,128)(2,1)} %copy-done.1), calls=%async_computation.2 | async-start | bytes 1572864 | tf_op jit(solution)/shard_map/all_to_all | solution.py:393
  169.9 27.3 %attend_back.1 = bf16[16,192,384]{2,1,0:T(8,128)(2,1)} custom-call(s32[3,8]{1,0:T(4,128)S(1)} %copy-done.4, s32[3,28]{1,0:T(4,128)S(1)} %fusion.58.pairs_ref, s32[1]{0:T(128)} %bitcast.count_ref, bf16[16,192,384]{2,1,0:T(8,128)(2,1)} %copy-done, bf16[16,64,384]{2,1,0:T(8,128)(2,1)S(1)} %all-to-all-done.1.grad_ref, bf16[16,64,384]{2,1,0:T(8,128)(2,1)S(1)} %copy-done.2, ...), custom_call_target="tpu_custom_call" | custom-call | flops 16000000000 | bytes 8388608 | tf_op jit(solution)/shard_map/attend_back/pallas_call | solution.py:293
  198.1 7.3 %all-to-all-start.3 = ((bf16[16,192,384]{2,1,0:T(8,128)(2,1)}), bf16[16,192,384]{2,1,0:T(8,128)(2,1)}, u32[]{:S(2)}, u32[]{:S(2)}) async-start(bf16[16,192,384]{2,1,0:T(8,128)(2,1)} %attend_back.1), calls=%async_computation.3 | async-start | bytes 4718592 | tf_op jit(solution)/shard_map/all_to_all | solution.py:409
  205.9 1.6 copy.28
  207.4 2.7 copy.29
  210.1 3.0 constant_dynamic-slice_fusion.1
  215.4 2.2 collective-permute-done.2
  217.7 3.1 convolution_convert_fusion.1
  220.8 7.4 %all-to-all-done.3 = bf16[16,192,384]{2,1,0:T(8,128)(2,1)} async-done(((bf16[16,192,384]{2,1,0:T(8,128)(2,1)}), bf16[16,192,384]{2,1,0:T(8,128)(2,1)}, u32[]{:S(2)}, u32[]{:S(2)}) %all-to-all-start.3) | async-done | bytes 2359328 | tf_op jit(solution)/shard_map/all_to_all | solution.py:409
  228.2 2.5 bitcast_reduce_fusion.1
  231.9 11.3 %all-to-all-start.5 = ((bf16[64,16,1024]{2,1,0:T(8,128)(2,1)}), bf16[64,16,1024]{2,1,0:T(8,128)(2,1)}, u32[]{:S(2)}, u32[]{:S(2)}) async-start(bf16[64,16,1024]{2,1,0:T(8,128)(2,1)} %bitcast.89), calls=%async_computation.5 | async-start | bytes 4194304 | tf_op jit(solution)/shard_map/all_to_all | solution.py:439
  244.6 4.1 %fusion.11 = bf16[384,2048]{1,0:T(8,128)(2,1)S(1)} fusion(bf16[1024,384]{1,0:T(8,128)(2,1)S(1)} %bitcast.96, bf16[2048,2560]{1,0:T(8,128)(2,1)} %all-gather.2.cloned.1.call-done), kind=kOutput, calls=%fused_computation.18 | convolution fusion | flops 1611399168 | bytes 6553600 | tf_op jit(solution)/shard_map/dot_general | solution.py:424
  249.9 8.1 %convolution_convert_fusion = bf16[1024,1536]{1,0:T(8,128)(2,1)S(1)} fusion(bf16[1536,384]{1,0:T(8,128)(2,1)S(1)} %collective-permute-done.3, bf16[256,384]{1,0:T(8,128)(2,1)S(1)} %bitcast.105, bf16[256,384]{1,0:T(8,128)(2,1)S(1)} %bitcast.103, bf16[1024,384]{1,0:T(8,128)(2,1)S(1)} %bitcast.87, bf16[1024,384]{1,0:T(8,128)(2,1)} %collective-permute-done, ...), kind=kOutput, calls=%fused_computation.6 | convolution fusion | flops 2430074880 | bytes 7077888 | tf_op jit(solution)/shard_map/dot_general | solution.py:413
  258.1 2.1 pad_maximum_fusion
  260.2 13.0 %all-to-all-done.5 = bf16[64,16,1024]{2,1,0:T(8,128)(2,1)} async-done(((bf16[64,16,1024]{2,1,0:T(8,128)(2,1)}), bf16[64,16,1024]{2,1,0:T(8,128)(2,1)}, u32[]{:S(2)}, u32[]{:S(2)}) %all-to-all-start.5) | async-done | bytes 2097184 | tf_op jit(solution)/shard_map/all_to_all | solution.py:439
  273.2 5.9 %all-to-all-start.4 = ((bf16[64,16,1664]{2,1,0:T(8,128)(2,1)}), bf16[64,16,1664]{2,1,0:T(8,128)(2,1)}, u32[]{:S(2)}, u32[]{:S(2)}) async-start(bf16[64,16,1664]{2,1,0:T(8,128)(2,1)} %pad_maximum_fusion), calls=%async_computation.4 | async-start | bytes 6815744 | tf_op jit(solution)/shard_map/all_to_all | solution.py:464
  279.1 5.2 %multiply_reduce_fusion = (f32[384]{0:T(512)S(1)}, f32[384,2048]{1,0:T(8,128)S(1)}) fusion(f32[384]{0:T(512)S(1)} %rsqrt_bitcast_fusion, bf16[3,128,2048]{2,1,0:T(8,128)(2,1)S(1)} %copy-done.5, f32[2048]{0:T(1024)S(1)} %copy-done.15, bf16[1536,384]{1,0:T(8,128)(2,1)S(1)} %pad_maximum_fusion.2, bf16[2048,2560]{1,0:T(8,128)(2,1)} %all-gather.2.cloned.1.call-done), kind=kOutput, calls=%fused_computation.13 | convolution fusion | flops 2419850752 | bytes 12200960 | tf_op jit(solution)/shard_map/dot_general | solution.py:465
  284.3 1.8 multiply_convert_fusion
  286.2 2.6 convert_reduce_fusion.1
  288.7 34.6 %all-to-all-done.4 = bf16[64,16,1664]{2,1,0:T(8,128)(2,1)} async-done(((bf16[64,16,1664]{2,1,0:T(8,128)(2,1)}), bf16[64,16,1664]{2,1,0:T(8,128)(2,1)}, u32[]{:S(2)}, u32[]{:S(2)}) %all-to-all-start.4) | async-done | bytes 3407904 | tf_op jit(solution)/shard_map/all_to_all | solution.py:464
  323.3 2.4 convert_reduce_fusion
  (107 shorter events, 16.3 us)
Async XLA Ops:
  7.2 78.7 %all-gather.2.cloned.1.call-start = ((), (), s32[]{:S(2)}) async-start(), calls=%async_computation.6 | async-start | bytes 10567680 | tf_op jit(solution)/shard_map/all_gather | solution.py:343
  94.6 5.3 %copy-start.4 = (s32[3,8]{1,0:T(4,128)S(1)}, s32[3,8]{1,0:T(4,128)}, u32[]{:S(2)}) copy-start(s32[3,8]{1,0:T(4,128)} %ends_ref.3) | copy-start | bytes 292
  94.6 6.2 %copy-start.20 = (s32[28]{0:T(128)S(1)}, s32[28]{0:T(128)}, u32[]{:S(2)}) copy-start(s32[28]{0:T(128)} %constant.92.clone) | copy-start | bytes 340
  94.6 7.2 %copy-start.19 = (s32[28]{0:T(128)S(1)}, s32[28]{0:T(128)}, u32[]{:S(2)}) copy-start(s32[28]{0:T(128)} %constant.103) | copy-start | bytes 340
  94.6 42.5 %all-to-all-start = ((bf16[16,192,384]{2,1,0:T(8,128)(2,1)}), bf16[16,192,384]{2,1,0:T(8,128)(2,1)S(1)}, u32[]{:S(2)}, u32[]{:S(2)}) async-start(bf16[16,192,384]{2,1,0:T(8,128)(2,1)} %pad_maximum_fusion.1), calls=%async_computation | async-start | bytes 4718592 | tf_op jit(solution)/shard_map/all_to_all | solution.py:382
  137.1 22.5 %copy-start = (bf16[16,192,384]{2,1,0:T(8,128)(2,1)}, bf16[16,192,384]{2,1,0:T(8,128)(2,1)S(1)}, u32[]{:S(2)}) copy-start(bf16[16,192,384]{2,1,0:T(8,128)(2,1)S(1)} %all-to-all-done.in_ref) | copy-start | bytes 7077892
  137.1 23.4 %all-to-all-start.1 = ((bf16[16,64,384]{2,1,0:T(8,128)(2,1)}), bf16[16,64,384]{2,1,0:T(8,128)(2,1)S(1)}, u32[]{:S(2)}, u32[]{:S(2)}) async-start(bf16[16,64,384]{2,1,0:T(8,128)(2,1)} %bitcast.97), calls=%async_computation.1 | async-start | bytes 1572864 | tf_op jit(solution)/shard_map/all_to_all | solution.py:386
  159.7 0.9 copy-start.1
  160.6 36.6 %all-to-all-start.2 = ((bf16[16,64,384]{2,1,0:T(8,128)(2,1)}), bf16[16,64,384]{2,1,0:T(8,128)(2,1)S(1)}, u32[]{:S(2)}, u32[]{:S(2)}) async-start(bf16[16,64,384]{2,1,0:T(8,128)(2,1)} %copy-done.1), calls=%async_computation.2 | async-start | bytes 1572864 | tf_op jit(solution)/shard_map/all_to_all | solution.py:393
  167.8 1.2 copy-start.2
  169.0 0.9 copy-start.3
  197.2 8.2 %copy-start.5 = (bf16[3,128,2048]{2,1,0:T(8,128)(2,1)S(1)}, bf16[3,128,2048]{2,1,0:T(8,128)(2,1)}, u32[]{:S(2)}) copy-start(bf16[3,128,2048]{2,1,0:T(8,128)(2,1)} %param.12) | copy-start | bytes 4718596
  197.2 8.2 %copy-start.15 = (f32[2048]{0:T(1024)S(1)}, f32[2048]{0:T(1024)}, u32[]{:S(2)}) copy-start(f32[2048]{0:T(1024)} %param.14) | copy-start | bytes 24580
  197.2 0.9 copy-start.8
  198.1 30.1 %all-to-all-start.3 = ((bf16[16,192,384]{2,1,0:T(8,128)(2,1)}), bf16[16,192,384]{2,1,0:T(8,128)(2,1)}, u32[]{:S(2)}, u32[]{:S(2)}) async-start(bf16[16,192,384]{2,1,0:T(8,128)(2,1)} %attend_back.1), calls=%async_computation.3 | async-start | bytes 4718592 | tf_op jit(solution)/shard_map/all_to_all | solution.py:409
  207.4 2.7 copy-start.6
  210.1 3.0 copy-start.9
  213.1 2.3 collective-permute-start.1
  213.1 4.5 %collective-permute-start.2 = (bf16[1024,384]{1,0:T(8,128)(2,1)S(1)}, bf16[1024,384]{1,0:T(8,128)(2,1)S(1)}, u32[]{:S(2)}, u32[]{:S(2)}) collective-permute-start(bf16[1024,384]{1,0:T(8,128)(2,1)S(1)} %bitcast.94), channel_id=1, source_target_pairs={{0,1},{1,0},{2,3},{3,2},{4,5},{5,4},{6,7},{7,6},{8,9},{9,8},{10,11... | collective-permute-start | bytes 2359304 | tf_op jit(solution)/shard_map/ppermute | solution.py:421
  213.6 35.9 %collective-permute-start = (bf16[1024,384]{1,0:T(8,128)(2,1)}, bf16[1024,384]{1,0:T(8,128)(2,1)}, u32[]{:S(2)}, u32[]{:S(2)}) collective-permute-start(bf16[1024,384]{1,0:T(8,128)(2,1)} %bitcast.16), channel_id=1, source_target_pairs={{0,1},{1,0},{2,3},{3,2},{4,5},{5,4},{6,7},{7,6},{8,9},{9,8},{10,11... | collective-permute-start | bytes 2359304 | tf_op jit(solution)/shard_map/ppermute | solution.py:360
  213.7 7.2 %copy-start.17 = (pred[3,3]{1,0:T(4,128)(4,1)}, pred[3,3]{1,0:T(4,128)(4,1)S(1)}, u32[]{:S(2)}) copy-start(pred[3,3]{1,0:T(4,128)(4,1)S(1)} %iota_compare_fusion.3) | copy-start | bytes 31
  231.9 41.3 %all-to-all-start.5 = ((bf16[64,16,1024]{2,1,0:T(8,128)(2,1)}), bf16[64,16,1024]{2,1,0:T(8,128)(2,1)}, u32[]{:S(2)}, u32[]{:S(2)}) async-start(bf16[64,16,1024]{2,1,0:T(8,128)(2,1)} %bitcast.89), calls=%async_computation.5 | async-start | bytes 4194304 | tf_op jit(solution)/shard_map/all_to_all | solution.py:439
  243.2 1.4 copy-start.10
  244.4 4.3 %copy-start.14 = (f32[24,2048]{1,0:T(8,128)S(1)}, f32[24,2048]{1,0:T(8,128)}, u32[]{:S(2)}) copy-start(f32[24,2048]{1,0:T(8,128)} %fusion.40) | copy-start | bytes 589828
  244.5 4.3 %copy-start.18 = (pred[3,3]{1,0:T(4,128)(4,1)S(1)}, pred[3,3]{1,0:T(4,128)(4,1)}, u32[]{:S(2)}) copy-start(pred[3,3]{1,0:T(4,128)(4,1)} %copy-done.17) | copy-start | bytes 31
  244.5 4.8 %copy-start.16 = (f32[2048]{0:T(1024)S(1)}, f32[2048]{0:T(1024)}, u32[]{:S(2)}) copy-start(f32[2048]{0:T(1024)} %param.19) | copy-start | bytes 24580
  244.5 5.4 %copy-start.11 = (bf16[64,1,16,384]{3,2,1,0:T(8,128)(2,1)S(1)}, bf16[64,1,16,384]{3,2,1,0:T(8,128)(2,1)}, u32[]{:S(2)}) copy-start(bf16[64,1,16,384]{3,2,1,0:T(8,128)(2,1)} %get-tuple-element.49) | copy-start | bytes 2359300
  244.5 5.4 %copy-start.12 = (bf16[4,64,384]{2,1,0:T(8,128)(2,1)S(1)}, bf16[4,64,384]{2,1,0:T(8,128)(2,1)}, u32[]{:S(2)}) copy-start(bf16[4,64,384]{2,1,0:T(8,128)(2,1)} %get-tuple-element.23) | copy-start | bytes 589828
  244.5 5.4 %copy-start.13 = (bf16[4,64,384]{2,1,0:T(8,128)(2,1)S(1)}, bf16[4,64,384]{2,1,0:T(8,128)(2,1)}, u32[]{:S(2)}) copy-start(bf16[4,64,384]{2,1,0:T(8,128)(2,1)} %get-tuple-element.24) | copy-start | bytes 589828
  244.5 5.0 %collective-permute-start.3 = (bf16[1536,384]{1,0:T(8,128)(2,1)S(1)}, bf16[1536,384]{1,0:T(8,128)(2,1)S(1)}, u32[]{:S(2)}, u32[]{:S(2)}) collective-permute-start(bf16[1536,384]{1,0:T(8,128)(2,1)S(1)} %pad_maximum_fusion.2), channel_id=1, source_target_pairs={{0,1},{1,0},{2,3},{3,2},{4,5},{5,4},{6,7},{7,6},{8,9},{9,8},{10,11... | collective-permute-start | bytes 3538952 | tf_op jit(solution)/shard_map/ppermute | solution.py:451
  248.8 1.1 copy-start.7
  273.2 50.1 %all-to-all-start.4 = ((bf16[64,16,1664]{2,1,0:T(8,128)(2,1)}), bf16[64,16,1664]{2,1,0:T(8,128)(2,1)}, u32[]{:S(2)}, u32[]{:S(2)}) async-start(bf16[64,16,1664]{2,1,0:T(8,128)(2,1)} %pad_maximum_fusion), calls=%async_computation.4 | async-start | bytes 6815744 | tf_op jit(solution)/shard_map/all_to_all | solution.py:464
Sparse Core Ops, SparseCore 0:
  11.7 74.0 all-gather.1

commit v3 on v2

v3 whole, which is shorter than its diff:
```python
import jax
import jax.numpy as jnp
from jax import lax
from jax.experimental import pallas as pl
from jax.experimental.pallas import tpu as pltpu
from jax.sharding import Mesh
from jax.sharding import PartitionSpec as P

HEADS = 16
KV_HEADS = 4
HEAD_DIM = 64
GROUP = HEADS // KV_HEADS
SLABS_HERE = 3
SET_OF = (0, 0, 1)
UNITS, SETS = 3, 2
HALF = HEAD_DIM // 2
BLOCK = 256

eps = 1e-05
base_theta = 500000.0


def rotation_tables(positions):
    freqs = base_theta ** (-(2.0 * jnp.arange(HALF, dtype=jnp.float32)) / HEAD_DIM)
    angles = positions.astype(jnp.float32)[None, :] * freqs[:, None]
    return jnp.cos(angles), jnp.sin(angles)


def pair_lists(end_rows, blocks):
    at = jnp.arange(blocks, dtype=jnp.int32) * BLOCK
    after = end_rows[:, None, :] + 1
    first = jnp.max(jnp.where(after <= at[None, :, None], after, 0), -1) // BLOCK
    codes = [(i, i - d) for d in range(1, blocks) for i in range(d, blocks)]
    query = jnp.array([i for i, _ in codes], jnp.int32)
    key = jnp.array([j for _, j in codes], jnp.int32)
    lowest = jnp.stack([first[:, i] for i, _ in codes], 1)
    valid = key[None] >= lowest
    place = jnp.cumsum(valid.astype(jnp.int32), 1) - 1
    slot = jnp.arange(len(codes), dtype=jnp.int32)
    chosen = valid[:, :, None] & (place[:, :, None] == slot)
    listed = jnp.sum(jnp.where(chosen, (query * blocks + key)[None, :, None], 0), 1)
    counts = jnp.sum(valid.astype(jnp.int32), 1)
    listed = jnp.where(slot[None] < counts[:, None], listed, blocks - 1)
    return listed, jnp.max(counts).reshape(1)


def block_of(ref, part, b):
    per = BLOCK // ref.shape[2]
    at = slice(part * HEAD_DIM, (part + 1) * HEAD_DIM)
    return jnp.concatenate([ref[b * per + r, at, :] for r in range(per)], axis=1)


def mask_of(starts, i, j):
    place = lax.broadcasted_iota(jnp.int32, (1, BLOCK), 1) + i * BLOCK
    key = lax.broadcasted_iota(jnp.int32, (BLOCK, BLOCK), 0) + j * BLOCK
    return (key >= starts) & (key <= place)


def starts_of(ends_ref, slab, b):
    place = lax.broadcasted_iota(jnp.int32, (1, BLOCK), 1) + b * BLOCK
    start = jnp.zeros((1, BLOCK), jnp.int32)
    for d in range(ends_ref.shape[1] - 1):
        after = ends_ref[slab, d] + 1
        start = jnp.where(place >= after, after, start)
    return start


def forward_kernel(
    ends_ref, pairs_ref, count_ref, in_ref, out_ref, stats_ref, q_s, k_s, vt_s, start_s, top_s, sum_s, acc_s
):
    n_src, _, rows = in_ref.shape
    per = BLOCK // rows
    blocks = n_src // per
    f32, bf16 = jnp.float32, jnp.bfloat16

    for b in range(blocks):
        for u in range(UNITS):
            q_s[u * blocks + b] = block_of(in_ref, u, b)
        for t in range(SETS):
            at = t * blocks + b
            k_s[at] = block_of(in_ref, UNITS + t, b).T
            vt_s[at] = block_of(in_ref, UNITS + SETS + t, b)
            start_s[at] = starts_of(ends_ref, t, b)

    def scores(u, i, j, mask):
        keys = k_s[SET_OF[u] * blocks + j]
        raw = jnp.dot(keys, q_s[u * blocks + i], preferred_element_type=f32)
        return jnp.where(mask, raw, -jnp.inf)

    def weighted(w, at):
        over_keys = (((0,), (1,)), ((), ()))
        return lax.dot_general(
            w.astype(bf16), vt_s[at], over_keys, preferred_element_type=f32
        ).T

    def diagonal(i, _):
        masks = [mask_of(start_s[t * blocks + i], i, i) for t in range(SETS)]
        done = []
        for u in range(UNITS):
            t = SET_OF[u]
            raw = scores(u, i, i, masks[t])
            top = jnp.max(raw, axis=0, keepdims=True)
            w = jnp.exp(raw - top)
            total = jnp.sum(w, axis=0, keepdims=True)
            done.append((u * blocks + i, top, total, weighted(w, t * blocks + i)))
        for at, top, total, acc in done:
            top_s[at], sum_s[at], acc_s[at] = top, total, acc
        return 0

    lax.fori_loop(0, blocks, diagonal, 0, unroll=True)

    def below(step, _):
        codes = [pairs_ref[t, step] for t in range(SETS)]
        places = [(lax.div(code, blocks), lax.rem(code, blocks)) for code in codes]
        masks = [mask_of(start_s[t * blocks + i], i, j) for t, (i, j) in enumerate(places)]
        done = []
        for u in range(UNITS):
            t = SET_OF[u]
            i, j = places[t]
            at = u * blocks + i
            raw = scores(u, i, j, masks[t])
            old = top_s[at]
            top = jnp.maximum(old, jnp.max(raw, axis=0, keepdims=True))
            fade = jnp.exp(old - top)
            w = jnp.exp(raw - top)
            total = sum_s[at] * fade + jnp.sum(w, axis=0, keepdims=True)
            acc = acc_s[at] * fade + weighted(w, t * blocks + j)
            done.append((at, top, total, acc))
        for at, top, total, acc in done:
            top_s[at], sum_s[at], acc_s[at] = top, total, acc
        return 0

    lax.fori_loop(0, count_ref[0], below, 0)

    for u in range(UNITS):
        for b in range(blocks):
            at = u * blocks + b
            inv = 1.0 / sum_s[at]
            stats_ref[at, 0:1, :] = top_s[at]
            stats_ref[at, 1:2, :] = inv
            ctx = (acc_s[at] * inv).astype(bf16)
            for r in range(per):
                out_ref[b * per + r, u * HEAD_DIM : (u + 1) * HEAD_DIM, :] = ctx[
                    :, r * rows : (r + 1) * rows
                ]


def backward_kernel(
    ends_ref,
    pairs_ref,
    count_ref,
    in_ref,
    grad_ref,
    ctx_ref,
    stats_ref,
    cos_ref,
    sin_ref,
    out_ref,
    q_s,
    kt_s,
    k_s,
    v_s,
    g_s,
    start_s,
    delta_s,
    dq_s,
    dk_s,
    dv_s,
):
    n_src, _, rows = in_ref.shape
    per = BLOCK // rows
    blocks = n_src // per
    f32, bf16 = jnp.float32, jnp.bfloat16
    hd = HEAD_DIM

    for b in range(blocks):
        for u in range(UNITS):
            at = u * blocks + b
            grad = block_of(grad_ref, u, b)
            ctx = block_of(ctx_ref, u, b)
            q_s[at] = block_of(in_ref, u, b)
            g_s[at] = grad
            delta_s[at] = jnp.sum(grad.astype(f32) * ctx.astype(f32), axis=0, keepdims=True)
        for t in range(SETS):
            at = t * blocks + b
            kt = block_of(in_ref, UNITS + t, b)
            kt_s[at] = kt
            k_s[at] = kt.T
            v_s[at] = block_of(in_ref, UNITS + SETS + t, b).T
            start_s[at] = starts_of(ends_ref, t, b)

    trans = (((1,), (1,)), ((), ()))

    def terms(places):
        masks = [mask_of(start_s[t * blocks + i], i, j) for t, (i, j) in enumerate(places)]
        dqs, dks, dvs = [], [None] * SETS, [None] * SETS
        for u in range(UNITS):
            t = SET_OF[u]
            i, j = places[t]
            qi, kj = u * blocks + i, t * blocks + j
            query, grad = q_s[qi], g_s[qi]
            raw = jnp.dot(k_s[kj], query, preferred_element_type=f32)
            raw = jnp.where(masks[t], raw, -jnp.inf)
            probs = jnp.exp(raw - stats_ref[qi, 0:1, :]) * stats_ref[qi, 1:2, :]
            dp = jnp.dot(v_s[kj], grad, preferred_element_type=f32)
            ds = (probs * (dp - delta_s[qi])).astype(bf16)
            dv = lax.dot_general(grad, probs.astype(bf16), trans, preferred_element_type=f32)
            dk = lax.dot_general(query, ds, trans, preferred_element_type=f32)
            dqs.append((qi, jnp.dot(kt_s[kj], ds, preferred_element_type=f32)))
            dks[t] = (kj, dk if dks[t] is None else dks[t][1] + dk)
            dvs[t] = (kj, dv if dvs[t] is None else dvs[t][1] + dv)
        return ((dq_s, dqs), (dk_s, dks), (dv_s, dvs))

    def diagonal(i, _):
        for ref, values in terms([(i, i)] * SETS):
            for at, value in values:
                ref[at] = value
        return 0

    lax.fori_loop(0, blocks, diagonal, 0, unroll=True)

    def below(step, _):
        codes = [pairs_ref[t, step] for t in range(SETS)]
        places = [(lax.div(code, blocks), lax.rem(code, blocks)) for code in codes]
        done = [
            (ref, at, ref[at] + value) for ref, values in terms(places) for at, value in values
        ]
        for ref, at, value in done:
            ref[at] = value
        return 0

    lax.fori_loop(0, count_ref[0], below, 0)

    def turned_back(grads, at, lanes, src, factor):
        x, y = grads[at, :HALF, lanes] * factor, grads[at, HALF:, lanes] * factor
        cosine, sine = cos_ref[src], sin_ref[src]
        return (x * cosine + y * sine).astype(bf16), (y * cosine - x * sine).astype(bf16)

    for b in range(blocks):
        for r in range(per):
            lanes, src = slice(r * rows, (r + 1) * rows), b * per + r
            for u in range(UNITS):
                x, y = turned_back(dq_s, u * blocks + b, lanes, src, hd**-0.5)
                out_ref[src, u * hd : u * hd + HALF, :] = x
                out_ref[src, u * hd + HALF : (u + 1) * hd, :] = y
            for t in range(SETS):
                at, to = t * blocks + b, UNITS + t
                x, y = turned_back(dk_s, at, lanes, src, 1.0)
                out_ref[src, to * hd : to * hd + HALF, :] = x
                out_ref[src, to * hd + HALF : (to + 1) * hd, :] = y
                to += SETS
                out_ref[src, to * hd : (to + 1) * hd, :] = dv_s[at, :, lanes].astype(bf16)


SMEM = pl.BlockSpec(memory_space=pltpu.SMEM)
VMEM = pl.BlockSpec(memory_space=pltpu.VMEM)
VMEM_LIMIT = 48 * 1024 * 1024


def attend(received, ends, pairs, count):
    n_src, _, rows = received.shape
    blocks = n_src * rows // BLOCK
    n, m = UNITS * blocks, SETS * blocks
    bf16, f32 = jnp.bfloat16, jnp.float32
    row = pltpu.VMEM((n, 1, BLOCK), f32)
    return pl.pallas_call(
        forward_kernel,
        out_shape=(
            jax.ShapeDtypeStruct((n_src, UNITS * HEAD_DIM, rows), bf16),
            jax.ShapeDtypeStruct((n, 2, BLOCK), f32),
        ),
        in_specs=[SMEM, SMEM, SMEM, VMEM],
        out_specs=(VMEM, VMEM),
        scratch_shapes=[
            pltpu.VMEM((n, HEAD_DIM, BLOCK), bf16),
            pltpu.VMEM((m, BLOCK, HEAD_DIM), bf16),
            pltpu.VMEM((m, HEAD_DIM, BLOCK), bf16),
            pltpu.VMEM((m, 1, BLOCK), jnp.int32),
            row,
            row,
            pltpu.VMEM((n, HEAD_DIM, BLOCK), f32),
        ],
        compiler_params=pltpu.CompilerParams(vmem_limit_bytes=VMEM_LIMIT),
        cost_estimate=pl.CostEstimate(
            flops=8 * 10**9, bytes_accessed=4 * 2**20, transcendentals=3 * 2**20
        ),
        name="attend",
    )(ends, pairs, count, received)


def attend_back(received, grads, context, stats, ends, pairs, count, cos_all, sin_all):
    n_src, _, rows = received.shape
    blocks = n_src * rows // BLOCK
    n, m = UNITS * blocks, SETS * blocks
    bf16, f32 = jnp.bfloat16, jnp.float32
    tall = pltpu.VMEM((m, BLOCK, HEAD_DIM), bf16)
    return pl.pallas_call(
        backward_kernel,
        out_shape=jax.ShapeDtypeStruct(received.shape, bf16),
        in_specs=[SMEM, SMEM, SMEM] + [VMEM] * 6,
        out_specs=VMEM,
        scratch_shapes=[
            pltpu.VMEM((n, HEAD_DIM, BLOCK), bf16),
            pltpu.VMEM((m, HEAD_DIM, BLOCK), bf16),
            tall,
            tall,
            pltpu.VMEM((n, HEAD_DIM, BLOCK), bf16),
            pltpu.VMEM((m, 1, BLOCK), jnp.int32),
            pltpu.VMEM((n, 1, BLOCK), f32),
            pltpu.VMEM((n, HEAD_DIM, BLOCK), f32),
            pltpu.VMEM((m, HEAD_DIM, BLOCK), f32),
            pltpu.VMEM((m, HEAD_DIM, BLOCK), f32),
        ],
        compiler_params=pltpu.CompilerParams(vmem_limit_bytes=VMEM_LIMIT),
        cost_estimate=pl.CostEstimate(
            flops=16 * 10**9, bytes_accessed=8 * 2**20, transcendentals=3 * 2**20
        ),
        name="attend_back",
    )(ends, pairs, count, received, grads, context, stats, cos_all, sin_all)


def to_units(heads):
    pairs = heads.reshape(HEADS // 2, 2, HEAD_DIM, -1)
    first, second, last = jnp.split(pairs, SLABS_HERE, axis=-1)
    return jnp.stack(
        [
            jnp.concatenate([own[:, 0], own[:, 1], last[:, e]], 1)
            for e, own in enumerate((first, second))
        ],
        1,
    )


def to_sets(heads):
    first, second, last = jnp.split(heads, SLABS_HERE, axis=-1)
    both = jnp.stack([jnp.concatenate([own, last], 1) for own in (first, second)], 1)
    return jnp.repeat(both, GROUP // 2, axis=0)


def from_units(units):
    rows = units.shape[-1]
    units = units.reshape(HEADS // 2, 2, UNITS, HEAD_DIM, rows)
    parts = [units[:, 0, :2], units[:, 1, :2], units[:, :, 2]]
    return jnp.concatenate(parts, -1).reshape(HEADS * HEAD_DIM, -1)


def from_sets(sets):
    rows = sets.shape[-1]
    sets = sets.astype(jnp.float32)
    sets = sets.reshape(KV_HEADS, GROUP // 2, 2, SETS, HEAD_DIM, rows)
    parts = [
        jnp.sum(sets[:, :, 0, 0], 1),
        jnp.sum(sets[:, :, 1, 0], 1),
        jnp.sum(sets[:, :, :, 1], (1, 2)),
    ]
    return jnp.concatenate(parts, -1).astype(jnp.bfloat16).reshape(KV_HEADS * HEAD_DIM, -1)


def on_device(
    tokens,
    segment_ids,
    end_rows,
    input_norm_gain,
    query_weight,
    key_weight,
    value_weight,
    out_weight,
    head_weight,
    branch_grad,
):
    del segment_ids
    bf16, f32 = jnp.bfloat16, jnp.float32
    n_ctx, n_x, n_core = (lax.axis_size(a) for a in ("ctx", "x", "core"))
    rank = lax.axis_index("ctx")
    core = lax.axis_index("core")
    slabs, rows, model = tokens.shape
    docs = end_rows.shape[1]
    tok = slabs * rows
    width = HEADS * HEAD_DIM
    kv_width = KV_HEADS * HEAD_DIM
    qkv = width + 2 * kv_width
    swap = [(c, n_core - 1 - c) for c in range(n_core)]

    weights = lax.all_gather(
        jnp.concatenate([query_weight, key_weight, value_weight, out_weight], 1),
        ("ctx", "x", "core"),
        axis=0,
        tiled=True,
    )

    flat = tokens.reshape(tok, model)
    grad_out = branch_grad.reshape(tok, model)
    wide = flat.astype(f32)
    inverse_norm = lax.rsqrt(jnp.mean(wide * wide, -1, keepdims=True) + eps)
    normed = (wide * inverse_norm * input_norm_gain).astype(bf16)

    split = grad_out.T.reshape(model // (16 * n_core), n_core, 16, tok)
    mine = lax.dynamic_index_in_dim(split, core, 1, keepdims=False).reshape(-1, tok)
    other = lax.dynamic_index_in_dim(split, 1 - core, 1, keepdims=False).reshape(-1, tok)
    grad_out_both = jnp.concatenate([mine, lax.ppermute(other, "core", swap)], 1)
    n_fsdp = n_x * n_core
    normed_rows = jnp.swapaxes(normed.T.reshape(n_ctx, n_fsdp, 16, tok), 0, 1)
    normed_rows = normed_rows.reshape(model, tok)

    first = rank * rows
    cos_all, sin_all = rotation_tables(jnp.arange(n_ctx * rows, dtype=jnp.int32))
    cos_here, sin_here = rotation_tables(first + jnp.arange(rows, dtype=jnp.int32))
    cos_here = jnp.tile(cos_here, (1, slabs))[None]
    sin_here = jnp.tile(sin_here, (1, slabs))[None]
    over = (((0,), (1,)), ((), ()))
    projected = lax.dot_general(weights[:, :qkv], normed, over, preferred_element_type=f32)
    turning = projected[: width + kv_width].reshape(HEADS + KV_HEADS, 2, HALF, tok)
    front, back = turning[:, 0], turning[:, 1]
    turned = jnp.concatenate(
        [front * cos_here - back * sin_here, back * cos_here + front * sin_here], 1
    )
    query = (turned[:HEADS] * (HEAD_DIM**-0.5)).astype(bf16)
    keys = turned[HEADS:].astype(bf16)
    values = projected[width + kv_width :].astype(bf16).reshape(KV_HEADS, HEAD_DIM, tok)
    send = jnp.concatenate([to_units(query), to_sets(keys), to_sets(values)], 2)
    send = send.reshape(HEADS, -1, rows)
    received = lax.all_to_all(send, "ctx", split_axis=0, concat_axis=0, tiled=True)
    context_grad = lax.dot_general(
        weights[:, qkv:], grad_out, over, preferred_element_type=f32
    ).astype(bf16)
    grads_in = lax.all_to_all(
        to_units(context_grad).reshape(HEADS, -1, rows), "ctx", split_axis=0, concat_axis=0, tiled=True
    )

    own = lax.dynamic_index_in_dim(end_rows, lax.rem(rank, 2), 0, keepdims=False)
    ends = jnp.stack([own, end_rows[SLABS_HERE - 1]], 0)
    pairs, count = pair_lists(ends, n_ctx * rows // BLOCK)
    context_head, stats = attend(received, ends, pairs, count)
    context_head, grads_in = lax.optimization_barrier((context_head, grads_in))
    context = lax.all_to_all(context_head, "ctx", split_axis=0, concat_axis=0, tiled=True)

    def by_source(table):
        return jnp.swapaxes(table.reshape(HALF, n_ctx, rows), 0, 1)

    results = attend_back(
        received,
        grads_in,
        context_head,
        stats,
        ends,
        pairs,
        count,
        by_source(cos_all),
        by_source(sin_all),
    )
    back_home = lax.all_to_all(results, "ctx", split_axis=0, concat_axis=0, tiled=True)
    last = (((1,), (1,)), ((), ()))

    context = from_units(context)
    context_other = lax.ppermute(context, "core", swap)
    partial_out = lax.dot_general(
        grad_out_both,
        jnp.concatenate([context, context_other], 1),
        last,
        preferred_element_type=f32,
    ).astype(bf16)

    branch = lax.dot_general(context, weights[:, qkv:], over, preferred_element_type=f32)
    branch = branch.astype(bf16)
    here = jnp.arange(slabs, dtype=jnp.int32)
    marks = (
        (end_rows[:, :, None, None] == first + jnp.arange(rows, dtype=jnp.int32))
        & (here[:, None, None, None] == here[:, None])
    ).astype(bf16)
    marks = marks.reshape(slabs * docs, tok)
    picked = jnp.dot(marks, flat, preferred_element_type=f32) + jnp.dot(
        marks, branch, preferred_element_type=f32
    )
    picked = picked * lax.rsqrt(jnp.mean(picked * picked, -1, keepdims=True) + eps)
    rewards = jnp.sum(picked * head_weight, -1).reshape(slabs, docs)
    hd = HEAD_DIM
    back_home, partial_out = lax.optimization_barrier((back_home, partial_out))
    pieces_out = lax.all_to_all(partial_out, "ctx", split_axis=0, concat_axis=0, tiled=True)
    edge = UNITS * hd
    dquery = from_units(back_home[:, :edge])
    dkey = from_sets(back_home[:, edge : edge + SETS * hd])
    dvalue = from_sets(back_home[:, edge + SETS * hd :])
    grads = jnp.concatenate([dquery, dkey, dvalue], 0)
    partial = lax.dot_general(normed_rows, grads, last, preferred_element_type=f32).astype(bf16)
    partial, grads, context = lax.optimization_barrier((partial, grads, context))
    summed = lax.psum_scatter(partial, ("x", "core"), scatter_dimension=0, tiled=True)
    summed, pieces_out = lax.optimization_barrier((summed, pieces_out))
    sums_out = jnp.sum(pieces_out.reshape(n_ctx, n_x, -1, width).astype(f32), 0)
    place = lax.axis_index("x")
    summed_out = lax.dynamic_index_in_dim(sums_out, place, 0, keepdims=False)
    for shift in range(1, n_x):
        target = lax.rem(place + shift, n_x)
        piece = lax.dynamic_index_in_dim(sums_out, target, 0, keepdims=False)
        around = [(c, (c + shift) % n_x) for c in range(n_x)]
        summed_out = summed_out + lax.ppermute(piece, "x", around)
    parts = []
    rest = rewards.reshape(-1)
    for _ in range(3):
        part = lax.reduce_precision(rest, 8, 7)
        parts.append(part)
        rest = rest - part
    riders = jnp.stack(parts, 0).astype(bf16)
    extra = 128
    riders = jnp.pad(riders, ((0, 16 - len(parts)), (0, extra - riders.shape[1])))
    summed = jnp.concatenate([summed, jnp.tile(riders, (n_ctx, 1))], 1)
    pieces = lax.all_to_all(summed, "ctx", split_axis=0, concat_axis=0, tiled=True)
    dnormed = lax.dot_general(grads, weights[:, :qkv], over, preferred_element_type=f32)
    scaled = dnormed * input_norm_gain
    centered = wide * inverse_norm
    grad_tokens = inverse_norm * (
        scaled - centered * jnp.mean(scaled * centered, -1, keepdims=True)
    )
    pieces = pieces.reshape(n_ctx, -1, qkv + extra)
    summed = jnp.sum(pieces[:, :, :qkv].astype(f32), 0)
    riders = pieces[:, : len(parts), qkv:]
    rewards = jnp.sum(riders[:, :, : slabs * docs].astype(f32), (0, 1)).reshape(slabs, docs)
    return (
        branch.reshape(tokens.shape),
        rewards,
        grad_tokens.astype(bf16).reshape(tokens.shape),
        summed[:, :width],
        summed[:, width : width + kv_width],
        summed[:, width + kv_width :],
        summed_out,
    )


def solution(mesh):
    n_ctx, n_fsdp = mesh.devices.shape
    chips = Mesh(mesh.devices.reshape(n_ctx, n_fsdp // 2, 2), ("ctx", "x", "core"))
    fsdp = ("x", "core")
    rows = P(("ctx", "x", "core"), None)
    acts = P(fsdp, "ctx", None)
    return jax.shard_map(
        on_device,
        mesh=chips,
        in_specs=(
            acts,
            P(fsdp, None),
            P(fsdp, None),
            P(),
            rows,
            rows,
            rows,
            rows,
            P(),
            acts,
        ),
        out_specs=(acts, P(fsdp, None), acts, rows, rows, rows, rows),
        check_vma=False,
    )
```

time: 335 us -> 294 us (0.88)
  waiting for transfers between devices: 160 us -> 132 us
  Pallas kernels: 45.9 us -> 30.7 us
    all_to_all x3, waiting for transfers between devices: 47.6 us -> 24.5 us  [the longest x1 20.5 us: on_device(): lax.all_to_all(partial_out, 'ctx', split_axis=0, concat_axis=0, tiled=True)]
    pallas_call x1, Pallas kernels: 27.3 us -> 18.5 us  [attend_back(): pl.pallas_call(backward_kernel, out_shape=jax.ShapeDtypeStruct(received.s...]
    pallas_call x1, Pallas kernels: 18.6 us -> 12.2 us  [attend(): pl.pallas_call(forward_kernel, out_shape=(jax.ShapeDtypeStruct((n_src, UN...]
    all_to_all x3, starting transfers between devices: 21.1 us -> 15.2 us  [the longest x1 6.8 us: on_device(): lax.all_to_all(summed, 'ctx', split_axis=0, concat_axis=0, tiled=True)]
    all_to_all x1, waiting for transfers between devices: 27.5 us -> 21.7 us  [on_device(): lax.all_to_all(send, 'ctx', split_axis=0, concat_axis=0, tiled=True)]
    reduce_scatter x0 -> x1, waiting for transfers between devices: none -> 5.05 us  [on_device(): lax.psum_scatter(partial, ('x', 'core'), scatter_dimension=0, tiled=True)]
    ppermute x3 -> x4, starting transfers between devices: 0.09 us -> 3.92 us  [the longest x3 3.92 us: on_device(): summed_out = summed_out + lax.ppermute(piece, 'x', around)]
    all_gather x1, waiting for transfers between devices: 75.1 us -> 71.6 us  [on_device(): lax.all_gather(jnp.concatenate([query_weight, key_weight, value_weight, o...]
  transfers between devices with their start and end apart: 11 -> 13, of which waited for: 7 -> 9; matrix products, arithmetic and copies ran while one was open for 16% -> 17% of each run, Pallas kernels for 14% -> 10%
where the time goes in v3:
time: 294 us; the launch traced here: 293 us
  waiting for transfers between devices  132 us (45%)
  starting transfers between devices  40.4 us (14%)
  matrix products  34.8 us (12%)
  Pallas kernels  30.7 us (10%)
  other arithmetic  22.8 us (8%)
  local copies, waits for them, and re-layouts  17.5 us (6%)
  between operations  14.7 us (5%)
    all_gather x1, waiting for transfers between devices, on_device(): lax.all_gather(jnp.concatenate([query_weight, key_weight, value_weight, o...  71.6 us
    all_to_all x1, waiting for transfers between devices, on_device(): lax.all_to_all(send, 'ctx', split_axis=0, concat_axis=0, tiled=True)  21.7 us
    all_to_all x1, waiting for transfers between devices, on_device(): lax.all_to_all(partial_out, 'ctx', split_axis=0, concat_axis=0, tiled=True)  20.5 us
    pallas_call x1, Pallas kernels, attend_back(): pl.pallas_call(backward_kernel, out_shape=jax.ShapeDtypeStruct(received.s...  18.5 us
    pallas_call x1, Pallas kernels, attend(): pl.pallas_call(forward_kernel, out_shape=(jax.ShapeDtypeStruct((n_src, UN...  12.2 us
    all_to_all x1, starting transfers between devices, on_device(): lax.all_to_all(results, 'ctx', split_axis=0, concat_axis=0, tiled=True)  8.78 us
    all_to_all x1, waiting for transfers between devices, on_device(): lax.all_to_all(results, 'ctx', split_axis=0, concat_axis=0, tiled=True)  7.69 us
    dot_general x1, matrix products, on_device(): lax.dot_general(grads, weights[:, :qkv], over, preferred_element_type=f32)  7.45 us
  transfers between devices with their start and end apart: 13, of which 9 were waited for; matrix products, arithmetic and copies ran while one was open for 17% of the time, Pallas kernels for 10%

profile of v3, /device:TPU:0, one launch (start us, length us, event | category | flops | bytes accessed | tf_op | source)
XLA Modules:
  0.0 292.9 jit_solution(7474406393137539224)
XLA Ops:
  7.2 1.6 pad_maximum_fusion.12
  12.3 1.8 multiply_reduce_fusion.1
  14.3 71.6 %all-gather.2.cloned.1.call-done = bf16[2048,2560]{1,0:T(8,128)(2,1)} async-done(((bf16[16,2560]{1,0:T(8,128)(2,1)}), bf16[2048,2560]{1,0:T(8,128)(2,1)}) %all-gather.2.cloned.1.call-update) | async-done | bytes 10485776 | tf_op jit(solution)/shard_map/all_gather | solution.py:384
  85.9 5.8 %fusion.2 = f32[1536,384]{1,0:T(8,128)S(1)} fusion(bf16[2048,2560]{1,0:T(8,128)(2,1)} %all-gather.2.cloned.1.call-done, bf16[384,2048]{1,0:T(8,128)(2,1)S(1)} %bitcast.167, f32[2048]{0:T(1024)S(1)} %copy-done.14, f32[384]{0:T(512)S(1)} %rsqrt_bitcast_fusion), kind=kOutput, calls=%fused_computation.3 | convolution fusion | flops 2419064832 | bytes 10233344 | tf_op jit(solution)/shard_map/dot_general | solution.py:411
  93.4 1.3 pad_maximum_fusion.1
  94.7 5.3 %all-to-all-start = ((bf16[16,448,128]{2,1,0:T(8,128)(2,1)}), bf16[16,448,128]{2,1,0:T(8,128)(2,1)S(1)}, u32[]{:S(2)}, u32[]{:S(2)}) async-start(bf16[16,448,128]{2,1,0:T(8,128)(2,1)} %pad_maximum_fusion.1), calls=%async_computation | async-start | bytes 3670016 | tf_op jit(solution)/shard_map/all_to_all | solution.py:422
  101.3 5.1 %fusion.28 = bf16[1024,384]{1,0:T(8,128)(2,1)S(1)} fusion(bf16[384,2048]{1,0:T(8,128)(2,1)} %bitcast.182, bf16[2048,2560]{1,0:T(8,128)(2,1)} %all-gather.2.cloned.1.call-done), kind=kOutput, calls=%fused_computation.38 | convolution fusion | flops 1611005952 | bytes 6553600 | tf_op jit(solution)/shard_map/dot_general | solution.py:423
  107.6 21.7 %all-to-all-done.in_ref = bf16[16,448,128]{2,1,0:T(8,128)(2,1)S(1)} async-done(((bf16[16,448,128]{2,1,0:T(8,128)(2,1)}), bf16[16,448,128]{2,1,0:T(8,128)(2,1)S(1)}, u32[]{:S(2)}, u32[]{:S(2)}) %all-to-all-start) | async-done | bytes 1835040 | tf_op jit(solution)/shard_map/all_to_all | solution.py:422
  129.3 3.8 %all-to-all-start.1 = ((bf16[16,192,128]{2,1,0:T(8,128)(2,1)}), bf16[16,192,128]{2,1,0:T(8,128)(2,1)S(1)}, u32[]{:S(2)}, u32[]{:S(2)}) async-start(bf16[16,192,128]{2,1,0:T(8,128)(2,1)} %bitcast.173), calls=%async_computation.1 | async-start | bytes 1572864 | tf_op jit(solution)/shard_map/all_to_all | solution.py:426
  133.1 12.2 %attend.1 = (bf16[16,192,128]{2,1,0:T(8,128)(2,1)}, f32[24,2,256]{2,1,0:T(2,128)S(1)}) custom-call(s32[2,8]{1,0:T(2,128)S(1)} %get-tuple-element.77.ends_ref, s32[2,28]{1,0:T(2,128)S(1)} %compare_select_fusion.pairs_ref, s32[1]{0:T(128)} %bitcast.count_ref, bf16[16,448,128]{2,1,0:T(8,128)(2,1)S(1)} %all-to-all-done.in_ref), custom_call_target="tpu_custom_call" | custom-call | flops 8000000000 | bytes 4194304 | tf_op jit(solution)/shard_map/attend/pallas_call | solution.py:266
  145.3 1.5 all-to-all-done.1.grad_ref
  146.8 6.7 %all-to-all-start.2 = ((bf16[16,192,128]{2,1,0:T(8,128)(2,1)}), bf16[16,192,128]{2,1,0:T(8,128)(2,1)}, u32[]{:S(2)}, u32[]{:S(2)}) async-start(bf16[16,192,128]{2,1,0:T(8,128)(2,1)} %get-tuple-element.18.ctx_ref), calls=%async_computation.2 | async-start | bytes 1572864 | tf_op jit(solution)/shard_map/all_to_all | solution.py:435
  153.6 18.5 %attend_back.1 = bf16[16,448,128]{2,1,0:T(8,128)(2,1)} custom-call(s32[2,8]{1,0:T(2,128)S(1)} %get-tuple-element.77.ends_ref, s32[2,28]{1,0:T(2,128)S(1)} %compare_select_fusion.pairs_ref, s32[1]{0:T(128)} %bitcast.count_ref, bf16[16,448,128]{2,1,0:T(8,128)(2,1)S(1)} %all-to-all-done.in_ref, bf16[16,192,128]{2,1,0:T(8,128)(2,1)S(1)} %all-to-all-done.1.grad_ref, ...), custom_call_target="tpu_custom_call" | custom-call | flops 16000000000 | bytes 8388608 | tf_op jit(solution)/shard_map/attend_back/pallas_call | solution.py:297
  172.0 8.8 %all-to-all-start.3 = ((bf16[16,448,128]{2,1,0:T(8,128)(2,1)}), bf16[16,448,128]{2,1,0:T(8,128)(2,1)S(1)}, u32[]{:S(2)}, u32[]{:S(2)}) async-start(bf16[16,448,128]{2,1,0:T(8,128)(2,1)} %attend_back.1), calls=%async_computation.3 | async-start | bytes 3670016 | tf_op jit(solution)/shard_map/all_to_all | solution.py:451
  180.9 1.9 copy.86
  187.9 1.6 fusion.31
  189.5 2.6 copy.84
  192.1 2.8 copy.85
  194.9 4.5 %convolution_convert_fusion.1 = bf16[1024,1024]{1,0:T(8,128)(2,1)} fusion(bf16[1024,384]{1,0:T(8,128)(2,1)} %collective-permute-done, bf16[1024,384]{1,0:T(8,128)(2,1)S(1)} %bitcast.205, bf16[1024,384]{1,0:T(8,128)(2,1)} %collective-permute-done.1, bf16[1024,128]{1,0:T(8,128)(2,1)S(1)} %bitcast.194, bf16[1024,128]{1,0:T(8,128)(2,1)S(1)} %bitcast.201, ...), kind=kOutput, calls=%fused_computation.22 | convolution fusion | flops 1621098496 | bytes 5242880 | tf_op jit(solution)/shard_map/dot_general | solution.py:456
  199.5 7.7 %all-to-all-done.3 = bf16[16,448,128]{2,1,0:T(8,128)(2,1)S(1)} async-done(((bf16[16,448,128]{2,1,0:T(8,128)(2,1)}), bf16[16,448,128]{2,1,0:T(8,128)(2,1)S(1)}, u32[]{:S(2)}, u32[]{:S(2)}) %all-to-all-start.3) | async-done | bytes 1835040 | tf_op jit(solution)/shard_map/all_to_all | solution.py:451
  209.5 6.2 %convolution_convert_fusion = bf16[2048,1536]{1,0:T(8,128)(2,1)} fusion(bf16[2048,384]{1,0:T(8,128)(2,1)S(1)} %bitcast.184, bf16[256,128]{1,0:T(8,128)(2,1)S(1)} %bitcast.207, bf16[256,128]{1,0:T(8,128)(2,1)S(1)} %bitcast.211, bf16[256,128]{1,0:T(8,128)(2,1)S(1)} %bitcast.209, bf16[256,128]{1,0:T(8,128)(2,1)S(1)} %bitcast.213, ...), kind=kOutput, calls=%fused_computation | convolution fusion | flops 2429681664 | bytes 9043968 | tf_op jit(solution)/shard_map/dot_general | solution.py:484
  217.5 4.2 %fusion.11 = bf16[384,2048]{1,0:T(8,128)(2,1)S(1)} fusion(bf16[2048,2560]{1,0:T(8,128)(2,1)} %all-gather.2.cloned.1.call-done, bf16[1024,128]{1,0:T(8,128)(2,1)S(1)} %bitcast.195, bf16[1024,128]{1,0:T(8,128)(2,1)} %bitcast.200, bf16[1024,128]{1,0:T(8,128)(2,1)} %bitcast.197), kind=kOutput, calls=%fused_computation.16 | convolution fusion | flops 1613758464 | bytes 6553600 | tf_op jit(solution)/shard_map/dot_general | solution.py:463
  221.8 4.6 %all-to-all-start.4 = ((bf16[16,64,1024]{2,1,0:T(8,128)(2,1)}), bf16[16,64,1024]{2,1,0:T(8,128)(2,1)}, u32[]{:S(2)}, u32[]{:S(2)}) async-start(bf16[16,64,1024]{2,1,0:T(8,128)(2,1)} %bitcast.179), calls=%async_computation.5 | async-start | bytes 4194304 | tf_op jit(solution)/shard_map/all_to_all | solution.py:478
  227.8 7.5 %multiply_reduce_fusion = (f32[384]{0:T(512)S(1)}, f32[384,2048]{1,0:T(8,128)}) fusion(f32[384]{0:T(512)S(1)} %rsqrt_bitcast_fusion, bf16[3,128,2048]{2,1,0:T(8,128)(2,1)S(1)} %copy-done.1, f32[2048]{0:T(1024)S(1)} %copy-done.14, bf16[1536,384]{1,0:T(8,128)(2,1)S(1)} %copy-done.4, bf16[2048,2560]{1,0:T(8,128)(2,1)} %all-gather.2.cloned.1.call-done), kind=kOutput, calls=%fused_computation.11 | convolution fusion | flops 2419850752 | bytes 12200960 | tf_op jit(solution)/shard_map/dot_general | solution.py:507
  235.3 20.5 %all-to-all-done.4 = bf16[16,64,1024]{2,1,0:T(8,128)(2,1)} async-done(((bf16[16,64,1024]{2,1,0:T(8,128)(2,1)}), bf16[16,64,1024]{2,1,0:T(8,128)(2,1)}, u32[]{:S(2)}, u32[]{:S(2)}) %all-to-all-start.4) | async-done | bytes 2097184 | tf_op jit(solution)/shard_map/all_to_all | solution.py:478
  255.7 5.0 %reduce-scatter.2.cloned.1.call-done = bf16[256,1536]{1,0:T(8,128)(2,1)} async-done(((bf16[2048,1536]{1,0:T(8,128)(2,1)}), bf16[256,1536]{1,0:T(8,128)(2,1)}) %reduce-scatter.2.cloned.1.call-update) | async-done | bytes 786448 | tf_op jit(solution)/shard_map/reduce_scatter | solution.py:486
  260.8 2.1 pad_maximum_fusion.2
  262.9 6.8 %all-to-all-start.5 = ((bf16[16,16,1664]{2,1,0:T(8,128)(2,1)}), bf16[16,16,1664]{2,1,0:T(8,128)(2,1)S(1)}, u32[]{:S(2)}, u32[]{:S(2)}) async-start(bf16[16,16,1664]{2,1,0:T(8,128)(2,1)} %pad_maximum_fusion.2), calls=%async_computation.6 | async-start | bytes 1703936 | tf_op jit(solution)/shard_map/all_to_all | solution.py:506
  269.7 2.0 convert_reduce_fusion
  271.8 3.0 %collective-permute-start.4 = (f32[16,1024]{1,0:T(8,128)S(1)}, f32[16,1024]{1,0:T(8,128)S(1)}, u32[]{:S(2)}, u32[]{:S(2)}) collective-permute-start(f32[16,1024]{1,0:T(8,128)S(1)} %get-tuple-element.59), channel_id=1, source_target_pairs={{0,6},{2,0},{4,2},{6,4},{1,7},{3,1},{5,3},{7,5},{8,14},{10,8},{12,... | collective-permute-start | bytes 196616 | tf_op jit(solution)/shard_map/ppermute | solution.py:495
  275.7 3.7 %multiply_convert_fusion = bf16[384,2048]{1,0:T(8,128)(2,1)} fusion(f32[384,2048]{1,0:T(8,128)} %get-tuple-element.84, f32[384]{0:T(512)S(1)} %broadcast_multiply_fusion, f32[384]{0:T(512)S(1)} %rsqrt_bitcast_fusion, bf16[3,128,2048]{2,1,0:T(8,128)(2,1)S(1)} %copy-done.1), kind=kLoop, calls=%fused_computation.10 | loop fusion | flops 4718592 | bytes 6294528 | tf_op jit(solution)/shard_map/convert_element_type | solution.py:520
  281.6 2.5 all-to-all-done.5
  (137 shorter events, 23.5 us)
Async XLA Ops:
  7.2 78.7 %copy-start = (bf16[3,128,2048]{2,1,0:T(8,128)(2,1)S(1)}, bf16[3,128,2048]{2,1,0:T(8,128)(2,1)}, u32[]{:S(2)}) copy-start(bf16[3,128,2048]{2,1,0:T(8,128)(2,1)} %param.12) | copy-start | bytes 4718596
  7.2 78.7 %copy-start.14 = (f32[2048]{0:T(1024)S(1)}, f32[2048]{0:T(1024)}, u32[]{:S(2)}) copy-start(f32[2048]{0:T(1024)} %param.14) | copy-start | bytes 24580
  7.2 78.7 %all-gather.2.cloned.1.call-start = ((), (), s32[]{:S(2)}) async-start(), calls=%async_computation.7 | async-start | bytes 10567680 | tf_op jit(solution)/shard_map/all_gather | solution.py:384
  94.7 5.4 %copy-start.17 = (s32[28]{0:T(128)S(1)}, s32[28]{0:T(128)}, u32[]{:S(2)}) copy-start(s32[28]{0:T(128)} %constant.120) | copy-start | bytes 340
  94.7 34.6 %all-to-all-start = ((bf16[16,448,128]{2,1,0:T(8,128)(2,1)}), bf16[16,448,128]{2,1,0:T(8,128)(2,1)S(1)}, u32[]{:S(2)}, u32[]{:S(2)}) async-start(bf16[16,448,128]{2,1,0:T(8,128)(2,1)} %pad_maximum_fusion.1), calls=%async_computation | async-start | bytes 3670016 | tf_op jit(solution)/shard_map/all_to_all | solution.py:422
  129.3 17.5 %all-to-all-start.1 = ((bf16[16,192,128]{2,1,0:T(8,128)(2,1)}), bf16[16,192,128]{2,1,0:T(8,128)(2,1)S(1)}, u32[]{:S(2)}, u32[]{:S(2)}) async-start(bf16[16,192,128]{2,1,0:T(8,128)(2,1)} %bitcast.173), calls=%async_computation.1 | async-start | bytes 1572864 | tf_op jit(solution)/shard_map/all_to_all | solution.py:426
  146.8 25.2 %all-to-all-start.2 = ((bf16[16,192,128]{2,1,0:T(8,128)(2,1)}), bf16[16,192,128]{2,1,0:T(8,128)(2,1)}, u32[]{:S(2)}, u32[]{:S(2)}) async-start(bf16[16,192,128]{2,1,0:T(8,128)(2,1)} %get-tuple-element.18.ctx_ref), calls=%async_computation.2 | async-start | bytes 1572864 | tf_op jit(solution)/shard_map/all_to_all | solution.py:435
  172.0 35.1 %all-to-all-start.3 = ((bf16[16,448,128]{2,1,0:T(8,128)(2,1)}), bf16[16,448,128]{2,1,0:T(8,128)(2,1)S(1)}, u32[]{:S(2)}, u32[]{:S(2)}) async-start(bf16[16,448,128]{2,1,0:T(8,128)(2,1)} %attend_back.1), calls=%async_computation.3 | async-start | bytes 3670016 | tf_op jit(solution)/shard_map/all_to_all | solution.py:451
  180.8 80.0 %reduce-scatter.2.cloned.1.call-start = ((), (), s32[]{:S(2)}) async-start(), calls=%async_computation.8 | async-start | bytes 7077888 | tf_op jit(solution)/shard_map/reduce_scatter | solution.py:486
  184.1 3.8 %copy-start.1 = (bf16[3,128,2048]{2,1,0:T(8,128)(2,1)S(1)}, bf16[3,128,2048]{2,1,0:T(8,128)(2,1)}, u32[]{:S(2)}) copy-start(bf16[3,128,2048]{2,1,0:T(8,128)(2,1)} %param.12) | copy-start | bytes 4718596
  184.1 10.8 %collective-permute-start = (bf16[1024,384]{1,0:T(8,128)(2,1)}, bf16[1024,384]{1,0:T(8,128)(2,1)}, u32[]{:S(2)}, u32[]{:S(2)}) collective-permute-start(bf16[1024,384]{1,0:T(8,128)(2,1)} %bitcast.46), channel_id=1, source_target_pairs={{0,1},{1,0},{2,3},{3,2},{4,5},{5,4},{6,7},{7,6},{8,9},{9,8},{10,11... | collective-permute-start | bytes 2359304 | tf_op jit(solution)/shard_map/ppermute | solution.py:400
  185.2 1.2 copy-start.5
  186.4 1.1 copy-start.8
  186.4 1.1 copy-start.10
  187.5 7.4 %collective-permute-start.1 = (bf16[1024,384]{1,0:T(8,128)(2,1)}, bf16[1024,384]{1,0:T(8,128)(2,1)}, u32[]{:S(2)}, u32[]{:S(2)}) collective-permute-start(bf16[1024,384]{1,0:T(8,128)(2,1)} %pad_maximum_fusion.5), channel_id=1, source_target_pairs={{0,1},{1,0},{2,3},{3,2},{4,5},{5,4},{6,7},{7,6},{8,9},{9,8},{10,11... | collective-permute-start | bytes 2359304 | tf_op jit(solution)/shard_map/ppermute | solution.py:455
  192.0 2.9 copy-start.6
  192.0 2.9 copy-start.9
  192.0 2.9 copy-start.11
  192.0 2.9 copy-start.12
  207.7 1.8 copy-start.2
  215.7 0.7 copy-start.16
  215.7 1.8 copy-start.7
  221.7 4.6 %copy-start.3 = (bf16[384,2048]{1,0:T(8,128)(2,1)}, bf16[384,2048]{1,0:T(8,128)(2,1)S(1)}, u32[]{:S(2)}) copy-start(bf16[384,2048]{1,0:T(8,128)(2,1)S(1)} %fusion.11) | copy-start | bytes 4718596
  221.7 4.6 %copy-start.13 = (f32[24,2048]{1,0:T(8,128)S(1)}, f32[24,2048]{1,0:T(8,128)}, u32[]{:S(2)}) copy-start(f32[24,2048]{1,0:T(8,128)} %fusion.39) | copy-start | bytes 589828
  221.7 5.1 %copy-start.15 = (f32[2048]{0:T(1024)S(1)}, f32[2048]{0:T(1024)}, u32[]{:S(2)}) copy-start(f32[2048]{0:T(1024)} %param.19) | copy-start | bytes 24580
  221.8 34.0 %all-to-all-start.4 = ((bf16[16,64,1024]{2,1,0:T(8,128)(2,1)}), bf16[16,64,1024]{2,1,0:T(8,128)(2,1)}, u32[]{:S(2)}, u32[]{:S(2)}) async-start(bf16[16,64,1024]{2,1,0:T(8,128)(2,1)} %bitcast.179), calls=%async_computation.5 | async-start | bytes 4194304 | tf_op jit(solution)/shard_map/all_to_all | solution.py:478
  226.4 1.4 copy-start.4
  262.9 21.1 %all-to-all-start.5 = ((bf16[16,16,1664]{2,1,0:T(8,128)(2,1)}), bf16[16,16,1664]{2,1,0:T(8,128)(2,1)S(1)}, u32[]{:S(2)}, u32[]{:S(2)}) async-start(bf16[16,16,1664]{2,1,0:T(8,128)(2,1)} %pad_maximum_fusion.2), calls=%async_computation.6 | async-start | bytes 1703936 | tf_op jit(solution)/shard_map/all_to_all | solution.py:506
  271.8 7.6 %collective-permute-start.4 = (f32[16,1024]{1,0:T(8,128)S(1)}, f32[16,1024]{1,0:T(8,128)S(1)}, u32[]{:S(2)}, u32[]{:S(2)}) collective-permute-start(f32[16,1024]{1,0:T(8,128)S(1)} %get-tuple-element.59), channel_id=1, source_target_pairs={{0,6},{2,0},{4,2},{6,4},{1,7},{3,1},{5,3},{7,5},{8,14},{10,8},{12,... | collective-permute-start | bytes 196616 | tf_op jit(solution)/shard_map/ppermute | solution.py:495
  274.7 5.9 %collective-permute-start.3 = (f32[16,1024]{1,0:T(8,128)S(1)}, f32[16,1024]{1,0:T(8,128)S(1)}, u32[]{:S(2)}, u32[]{:S(2)}) collective-permute-start(f32[16,1024]{1,0:T(8,128)S(1)} %get-tuple-element.60), channel_id=1, source_target_pairs={{0,4},{2,6},{4,0},{6,2},{1,5},{3,7},{5,1},{7,3},{8,12},{10,14},{12... | collective-permute-start | bytes 196616 | tf_op jit(solution)/shard_map/ppermute | solution.py:495
  274.7 6.2 %collective-permute-start.2 = (f32[16,1024]{1,0:T(8,128)S(1)}, f32[16,1024]{1,0:T(8,128)S(1)}, u32[]{:S(2)}, u32[]{:S(2)}) collective-permute-start(f32[16,1024]{1,0:T(8,128)S(1)} %get-tuple-element.58), channel_id=1, source_target_pairs={{0,2},{2,4},{4,6},{6,0},{1,3},{3,5},{5,7},{7,1},{8,10},{10,12},{12... | collective-permute-start | bytes 196616 | tf_op jit(solution)/shard_map/ppermute | solution.py:495
Sparse Core Ops, SparseCore 0:
  11.7 74.0 all-gather.1
  215.9 44.8 reduce-scatter.1

commit v4 on v3

--- a/solution.py
+++ b/solution.py
@@ -13,6 +13,7 @@
 SLABS_HERE = 3
 SET_OF = (0, 0, 1)
 UNITS, SETS = 3, 2
+STEPS, BACK_STEPS = 2, 1
 HALF = HEAD_DIM // 2
 BLOCK = 256
 
@@ -26,7 +27,7 @@
     return jnp.cos(angles), jnp.sin(angles)
 
 
-def pair_lists(end_rows, blocks):
+def pair_lists(end_rows, blocks, steps):
     at = jnp.arange(blocks, dtype=jnp.int32) * BLOCK
     after = end_rows[:, None, :] + 1
     first = jnp.max(jnp.where(after <= at[None, :, None], after, 0), -1) // BLOCK
@@ -35,13 +36,21 @@
     key = jnp.array([j for _, j in codes], jnp.int32)
     lowest = jnp.stack([first[:, i] for i, _ in codes], 1)
     valid = key[None] >= lowest
-    place = jnp.cumsum(valid.astype(jnp.int32), 1) - 1
-    slot = jnp.arange(len(codes), dtype=jnp.int32)
+    places, total = [], jnp.zeros((end_rows.shape[0], 1), jnp.int32)
+    at = 0
+    for d in range(1, blocks):
+        here = valid[:, at : at + blocks - d].astype(jnp.int32)
+        places.append(total + jnp.cumsum(here, 1) - 1)
+        number = jnp.sum(here, 1, keepdims=True)
+        total = total + (number + steps - 1) // steps * steps
+        at += blocks - d
+    place = jnp.concatenate(places, 1)
+    slot = jnp.arange(len(codes) + steps * blocks, dtype=jnp.int32)
     chosen = valid[:, :, None] & (place[:, :, None] == slot)
-    listed = jnp.sum(jnp.where(chosen, (query * blocks + key)[None, :, None], 0), 1)
-    counts = jnp.sum(valid.astype(jnp.int32), 1)
-    listed = jnp.where(slot[None] < counts[:, None], listed, blocks - 1)
-    return listed, jnp.max(counts).reshape(1)
+    code = (query * blocks + key)[None, :, None]
+    filled = jnp.any(chosen, 1)
+    listed = jnp.where(filled, jnp.sum(jnp.where(chosen, code, 0), 1), blocks - 1)
+    return listed, (jnp.max(total) // steps).reshape(1)
 
 
 def block_of(ref, part, b):
@@ -110,12 +119,14 @@
     lax.fori_loop(0, blocks, diagonal, 0, unroll=True)
 
     def below(step, _):
-        codes = [pairs_ref[t, step] for t in range(SETS)]
-        places = [(lax.div(code, blocks), lax.rem(code, blocks)) for code in codes]
-        masks = [mask_of(start_s[t * blocks + i], i, j) for t, (i, j) in enumerate(places)]
         done = []
-        for u in range(UNITS):
+        for n in range(STEPS * UNITS):
+            u = n % UNITS
             t = SET_OF[u]
+            if u == 0:
+                codes = [pairs_ref[t, step * STEPS + n // UNITS] for t in range(SETS)]
+                places = [(lax.div(code, blocks), lax.rem(code, blocks)) for code in codes]
+                masks = [mask_of(start_s[t * blocks + i], i, j) for t, (i, j) in enumerate(places)]
             i, j = places[t]
             at = u * blocks + i
             raw = scores(u, i, j, masks[t])
@@ -220,11 +231,13 @@
     lax.fori_loop(0, blocks, diagonal, 0, unroll=True)
 
     def below(step, _):
-        codes = [pairs_ref[t, step] for t in range(SETS)]
-        places = [(lax.div(code, blocks), lax.rem(code, blocks)) for code in codes]
-        done = [
-            (ref, at, ref[at] + value) for ref, values in terms(places) for at, value in values
-        ]
+        done = []
+        for n in range(BACK_STEPS):
+            codes = [pairs_ref[t, step * BACK_STEPS + n] for t in range(SETS)]
+            places = [(lax.div(code, blocks), lax.rem(code, blocks)) for code in codes]
+            done += [
+                (ref, at, ref[at] + value) for ref, values in terms(places) for at, value in values
+            ]
         for ref, at, value in done:
             ref[at] = value
         return 0
@@ -429,7 +442,9 @@
 
     own = lax.dynamic_index_in_dim(end_rows, lax.rem(rank, 2), 0, keepdims=False)
     ends = jnp.stack([own, end_rows[SLABS_HERE - 1]], 0)
-    pairs, count = pair_lists(ends, n_ctx * rows // BLOCK)
+    blocks = n_ctx * rows // BLOCK
+    pairs, count = pair_lists(ends, blocks, STEPS)
+    back_pairs, back_count = pair_lists(ends, blocks, BACK_STEPS)
     context_head, stats = attend(received, ends, pairs, count)
     context_head, grads_in = lax.optimization_barrier((context_head, grads_in))
     context = lax.all_to_all(context_head, "ctx", split_axis=0, concat_axis=0, tiled=True)
@@ -443,8 +458,8 @@
         context_head,
         stats,
         ends,
-        pairs,
-        count,
+        back_pairs,
+        back_count,
         by_source(cos_all),
         by_source(sin_all),
     )

time: 294 us -> 294 us (level); the launches traced: 293 us -> 296 us
  other arithmetic: 22.8 us -> 27.1 us
  starting transfers between devices: 40.4 us -> 36.1 us
    reduce_scatter x1, waiting for transfers between devices: 5.05 us -> 15.5 us  [on_device(): lax.psum_scatter(partial, ('x', 'core'), scatter_dimension=0, tiled=True)]
    all_gather x1, waiting for transfers between devices: 71.6 us -> 63.3 us  [on_device(): lax.all_gather(jnp.concatenate([query_weight, key_weight, value_weight, o...]
  transfers between devices with their start and end apart: 13 -> 13, of which waited for: 9 -> 9; matrix products, arithmetic and copies ran while one was open for 17% -> 19% of each run, Pallas kernels for 10% -> 10%
where the time goes in v4:
time: 294 us; the launch traced here: 296 us
  waiting for transfers between devices  132 us (45%)
  starting transfers between devices  36.1 us (12%)
  matrix products  34.7 us (12%)
  Pallas kernels  30.6 us (10%)
  other arithmetic  27.1 us (9%)
  local copies, waits for them, and re-layouts  18.3 us (6%)
  between operations  17.3 us (6%)
    all_gather x1, waiting for transfers between devices, on_device(): lax.all_gather(jnp.concatenate([query_weight, key_weight, value_weight, o...  63.3 us
    all_to_all x1, waiting for transfers between devices, on_device(): lax.all_to_all(send, 'ctx', split_axis=0, concat_axis=0, tiled=True)  21.9 us
    pallas_call x1, Pallas kernels, attend_back(): pl.pallas_call(backward_kernel, out_shape=jax.ShapeDtypeStruct(received.s...  19.5 us
    all_to_all x1, waiting for transfers between devices, on_device(): lax.all_to_all(partial_out, 'ctx', split_axis=0, concat_axis=0, tiled=True)  18.5 us
    reduce_scatter x1, waiting for transfers between devices, on_device(): lax.psum_scatter(partial, ('x', 'core'), scatter_dimension=0, tiled=True)  15.5 us
    pallas_call x1, Pallas kernels, attend(): pl.pallas_call(forward_kernel, out_shape=(jax.ShapeDtypeStruct((n_src, UN...  11.2 us
    dot_general x1, matrix products, on_device(): lax.dot_general(grads, weights[:, :qkv], over, preferred_element_type=f32)  7.49 us
    all_to_all x1, starting transfers between devices, on_device(): lax.all_to_all(results, 'ctx', split_axis=0, concat_axis=0, tiled=True)  7.17 us
  transfers between devices with their start and end apart: 13, of which 9 were waited for; matrix products, arithmetic and copies ran while one was open for 19% of the time, Pallas kernels for 10%

profile of v4, /device:TPU:0, one launch (start us, length us, event | category | flops | bytes accessed | tf_op | source)
XLA Modules:
  0.0 296.2 jit_solution(3692592844843721841)
XLA Ops:
  7.2 1.6 pad_maximum_fusion.12
  20.5 1.8 multiply_reduce_fusion.1
  22.5 63.3 %all-gather.2.cloned.1.call-done = bf16[2048,2560]{1,0:T(8,128)(2,1)} async-done(((bf16[16,2560]{1,0:T(8,128)(2,1)}), bf16[2048,2560]{1,0:T(8,128)(2,1)}) %all-gather.2.cloned.1.call-update) | async-done | bytes 10485776 | tf_op jit(solution)/shard_map/all_gather | solution.py:397
  85.9 5.8 %fusion.2 = f32[1536,384]{1,0:T(8,128)S(1)} fusion(bf16[2048,2560]{1,0:T(8,128)(2,1)} %all-gather.2.cloned.1.call-done, bf16[384,2048]{1,0:T(8,128)(2,1)S(1)} %bitcast.182, f32[2048]{0:T(1024)S(1)} %copy-done.14, f32[384]{0:T(512)S(1)} %rsqrt_bitcast_fusion), kind=kOutput, calls=%fused_computation.3 | convolution fusion | flops 2419064832 | bytes 10233344 | tf_op jit(solution)/shard_map/dot_general | solution.py:424
  93.4 1.4 pad_maximum_fusion.1
  94.7 5.2 %all-to-all-start = ((bf16[16,448,128]{2,1,0:T(8,128)(2,1)}), bf16[16,448,128]{2,1,0:T(8,128)(2,1)S(1)}, u32[]{:S(2)}, u32[]{:S(2)}) async-start(bf16[16,448,128]{2,1,0:T(8,128)(2,1)} %pad_maximum_fusion.1), calls=%async_computation | async-start | bytes 3670016 | tf_op jit(solution)/shard_map/all_to_all | solution.py:435
  100.9 5.1 %fusion.28 = bf16[1024,384]{1,0:T(8,128)(2,1)S(1)} fusion(bf16[384,2048]{1,0:T(8,128)(2,1)} %bitcast.197, bf16[2048,2560]{1,0:T(8,128)(2,1)} %all-gather.2.cloned.1.call-done), kind=kOutput, calls=%fused_computation.38 | convolution fusion | flops 1611005952 | bytes 6553600 | tf_op jit(solution)/shard_map/dot_general | solution.py:436
  107.2 21.9 %all-to-all-done.in_ref = bf16[16,448,128]{2,1,0:T(8,128)(2,1)S(1)} async-done(((bf16[16,448,128]{2,1,0:T(8,128)(2,1)}), bf16[16,448,128]{2,1,0:T(8,128)(2,1)S(1)}, u32[]{:S(2)}, u32[]{:S(2)}) %all-to-all-start) | async-done | bytes 1835040 | tf_op jit(solution)/shard_map/all_to_all | solution.py:435
  129.2 3.8 %all-to-all-start.1 = ((bf16[16,192,128]{2,1,0:T(8,128)(2,1)}), bf16[16,192,128]{2,1,0:T(8,128)(2,1)S(1)}, u32[]{:S(2)}, u32[]{:S(2)}) async-start(bf16[16,192,128]{2,1,0:T(8,128)(2,1)} %bitcast.188), calls=%async_computation.1 | async-start | bytes 1572864 | tf_op jit(solution)/shard_map/all_to_all | solution.py:439
  133.0 11.2 %attend.1 = (bf16[16,192,128]{2,1,0:T(8,128)(2,1)}, f32[24,2,256]{2,1,0:T(2,128)S(1)}) custom-call(s32[2,8]{1,0:T(2,128)S(1)} %get-tuple-element.104.ends_ref, s32[2,44]{1,0:T(2,128)S(1)} %broadcast_select_fusion.1.pairs_ref, s32[1]{0:T(128)} %bitcast.6.count_ref, bf16[16,448,128]{2,1,0:T(8,128)(2,1)S(1)} %all-to-all-done.in_ref), custom_call_target="tpu_custom_call" | custom-call | flops 8000000000 | bytes 4194304 | tf_op jit(solution)/shard_map/attend/pallas_call | solution.py:279
  144.2 2.5 all-to-all-done.1.grad_ref
  146.7 4.5 %all-to-all-start.2 = ((bf16[16,192,128]{2,1,0:T(8,128)(2,1)}), bf16[16,192,128]{2,1,0:T(8,128)(2,1)}, u32[]{:S(2)}, u32[]{:S(2)}) async-start(bf16[16,192,128]{2,1,0:T(8,128)(2,1)} %get-tuple-element.18.ctx_ref), calls=%async_computation.2 | async-start | bytes 1572864 | tf_op jit(solution)/shard_map/all_to_all | solution.py:450
  151.2 19.5 %attend_back.1 = bf16[16,448,128]{2,1,0:T(8,128)(2,1)} custom-call(s32[2,8]{1,0:T(2,128)S(1)} %get-tuple-element.104.ends_ref, s32[2,36]{1,0:T(2,128)S(1)} %broadcast_select_fusion.pairs_ref, s32[1]{0:T(128)} %bitcast.50.count_ref, bf16[16,448,128]{2,1,0:T(8,128)(2,1)S(1)} %all-to-all-done.in_ref, bf16[16,192,128]{2,1,0:T(8,128)(2,1)S(1)} %all-to-all-done.1.grad_ref, ...), custom_call_target="tpu_custom_call" | custom-call | flops 16000000000 | bytes 8388608 | tf_op jit(solution)/shard_map/attend_back/pallas_call | solution.py:310
  170.7 7.2 %all-to-all-start.3 = ((bf16[16,448,128]{2,1,0:T(8,128)(2,1)}), bf16[16,448,128]{2,1,0:T(8,128)(2,1)S(1)}, u32[]{:S(2)}, u32[]{:S(2)}) async-start(bf16[16,448,128]{2,1,0:T(8,128)(2,1)} %attend_back.1), calls=%async_computation.3 | async-start | bytes 3670016 | tf_op jit(solution)/shard_map/all_to_all | solution.py:466
  177.9 1.9 copy.192
  184.9 1.6 fusion.31
  186.4 2.6 copy.186
  189.0 2.8 copy.187
  191.9 4.6 %convolution_convert_fusion.1 = bf16[1024,1024]{1,0:T(8,128)(2,1)} fusion(bf16[1024,384]{1,0:T(8,128)(2,1)} %collective-permute-done, bf16[1024,384]{1,0:T(8,128)(2,1)S(1)} %bitcast.220, bf16[1024,384]{1,0:T(8,128)(2,1)} %collective-permute-done.1, bf16[1024,128]{1,0:T(8,128)(2,1)S(1)} %bitcast.209, bf16[1024,128]{1,0:T(8,128)(2,1)S(1)} %bitcast.216, ...), kind=kOutput, calls=%fused_computation.22 | convolution fusion | flops 1621098496 | bytes 5242880 | tf_op jit(solution)/shard_map/dot_general | solution.py:471
  196.5 5.6 %all-to-all-done.3 = bf16[16,448,128]{2,1,0:T(8,128)(2,1)S(1)} async-done(((bf16[16,448,128]{2,1,0:T(8,128)(2,1)}), bf16[16,448,128]{2,1,0:T(8,128)(2,1)S(1)}, u32[]{:S(2)}, u32[]{:S(2)}) %all-to-all-start.3) | async-done | bytes 1835040 | tf_op jit(solution)/shard_map/all_to_all | solution.py:466
  204.4 6.1 %convolution_convert_fusion = bf16[2048,1536]{1,0:T(8,128)(2,1)} fusion(bf16[2048,384]{1,0:T(8,128)(2,1)S(1)} %bitcast.199, bf16[256,128]{1,0:T(8,128)(2,1)S(1)} %bitcast.222, bf16[256,128]{1,0:T(8,128)(2,1)S(1)} %bitcast.226, bf16[256,128]{1,0:T(8,128)(2,1)S(1)} %bitcast.224, bf16[256,128]{1,0:T(8,128)(2,1)S(1)} %bitcast.228, ...), kind=kOutput, calls=%fused_computation | convolution fusion | flops 2429681664 | bytes 9043968 | tf_op jit(solution)/shard_map/dot_general | solution.py:499
  212.4 4.2 %fusion.11 = bf16[384,2048]{1,0:T(8,128)(2,1)S(1)} fusion(bf16[2048,2560]{1,0:T(8,128)(2,1)} %all-gather.2.cloned.1.call-done, bf16[1024,128]{1,0:T(8,128)(2,1)S(1)} %bitcast.210, bf16[1024,128]{1,0:T(8,128)(2,1)} %bitcast.215, bf16[1024,128]{1,0:T(8,128)(2,1)} %bitcast.212), kind=kOutput, calls=%fused_computation.16 | convolution fusion | flops 1613758464 | bytes 6553600 | tf_op jit(solution)/shard_map/dot_general | solution.py:478
  216.6 4.6 %all-to-all-start.4 = ((bf16[16,64,1024]{2,1,0:T(8,128)(2,1)}), bf16[16,64,1024]{2,1,0:T(8,128)(2,1)}, u32[]{:S(2)}, u32[]{:S(2)}) async-start(bf16[16,64,1024]{2,1,0:T(8,128)(2,1)} %bitcast.194), calls=%async_computation.5 | async-start | bytes 4194304 | tf_op jit(solution)/shard_map/all_to_all | solution.py:493
  222.5 7.5 %multiply_reduce_fusion = (f32[384]{0:T(512)S(1)}, f32[384,2048]{1,0:T(8,128)}) fusion(f32[384]{0:T(512)S(1)} %rsqrt_bitcast_fusion, bf16[3,128,2048]{2,1,0:T(8,128)(2,1)S(1)} %copy-done.1, f32[2048]{0:T(1024)S(1)} %copy-done.14, bf16[1536,384]{1,0:T(8,128)(2,1)S(1)} %copy-done.4, bf16[2048,2560]{1,0:T(8,128)(2,1)} %all-gather.2.cloned.1.call-done), kind=kOutput, calls=%fused_computation.11 | convolution fusion | flops 2419850752 | bytes 12200960 | tf_op jit(solution)/shard_map/dot_general | solution.py:522
  230.0 18.5 %all-to-all-done.4 = bf16[16,64,1024]{2,1,0:T(8,128)(2,1)} async-done(((bf16[16,64,1024]{2,1,0:T(8,128)(2,1)}), bf16[16,64,1024]{2,1,0:T(8,128)(2,1)}, u32[]{:S(2)}, u32[]{:S(2)}) %all-to-all-start.4) | async-done | bytes 2097184 | tf_op jit(solution)/shard_map/all_to_all | solution.py:493
  248.5 15.5 %reduce-scatter.2.cloned.1.call-done = bf16[256,1536]{1,0:T(8,128)(2,1)} async-done(((bf16[2048,1536]{1,0:T(8,128)(2,1)}), bf16[256,1536]{1,0:T(8,128)(2,1)}) %reduce-scatter.2.cloned.1.call-update) | async-done | bytes 786448 | tf_op jit(solution)/shard_map/reduce_scatter | solution.py:501
  264.0 2.1 pad_maximum_fusion.2
  266.1 6.9 %all-to-all-start.5 = ((bf16[16,16,1664]{2,1,0:T(8,128)(2,1)}), bf16[16,16,1664]{2,1,0:T(8,128)(2,1)S(1)}, u32[]{:S(2)}, u32[]{:S(2)}) async-start(bf16[16,16,1664]{2,1,0:T(8,128)(2,1)} %pad_maximum_fusion.2), calls=%async_computation.6 | async-start | bytes 1703936 | tf_op jit(solution)/shard_map/all_to_all | solution.py:521
  273.0 2.0 convert_reduce_fusion
  275.0 2.5 collective-permute-start.4
  278.5 3.7 %multiply_convert_fusion = bf16[384,2048]{1,0:T(8,128)(2,1)} fusion(f32[384,2048]{1,0:T(8,128)} %get-tuple-element.117, f32[384]{0:T(512)S(1)} %broadcast_multiply_fusion, f32[384]{0:T(512)S(1)} %rsqrt_bitcast_fusion, bf16[3,128,2048]{2,1,0:T(8,128)(2,1)S(1)} %copy-done.1), kind=kLoop, calls=%fused_computation.10 | loop fusion | flops 4718592 | bytes 6294528 | tf_op jit(solution)/shard_map/convert_element_type | solution.py:535
  284.4 2.9 all-to-all-done.5
  (172 shorter events, 28.6 us)
Async XLA Ops:
  7.2 78.7 %copy-start = (bf16[3,128,2048]{2,1,0:T(8,128)(2,1)S(1)}, bf16[3,128,2048]{2,1,0:T(8,128)(2,1)}, u32[]{:S(2)}) copy-start(bf16[3,128,2048]{2,1,0:T(8,128)(2,1)} %param.14) | copy-start | bytes 4718596
  7.2 78.7 %copy-start.14 = (f32[2048]{0:T(1024)S(1)}, f32[2048]{0:T(1024)}, u32[]{:S(2)}) copy-start(f32[2048]{0:T(1024)} %param.16) | copy-start | bytes 24580
  7.2 78.7 %all-gather.2.cloned.1.call-start = ((), (), s32[]{:S(2)}) async-start(), calls=%async_computation.7 | async-start | bytes 10567680 | tf_op jit(solution)/shard_map/all_gather | solution.py:397
  94.7 34.5 %all-to-all-start = ((bf16[16,448,128]{2,1,0:T(8,128)(2,1)}), bf16[16,448,128]{2,1,0:T(8,128)(2,1)S(1)}, u32[]{:S(2)}, u32[]{:S(2)}) async-start(bf16[16,448,128]{2,1,0:T(8,128)(2,1)} %pad_maximum_fusion.1), calls=%async_computation | async-start | bytes 3670016 | tf_op jit(solution)/shard_map/all_to_all | solution.py:435
  129.2 17.5 %all-to-all-start.1 = ((bf16[16,192,128]{2,1,0:T(8,128)(2,1)}), bf16[16,192,128]{2,1,0:T(8,128)(2,1)S(1)}, u32[]{:S(2)}, u32[]{:S(2)}) async-start(bf16[16,192,128]{2,1,0:T(8,128)(2,1)} %bitcast.188), calls=%async_computation.1 | async-start | bytes 1572864 | tf_op jit(solution)/shard_map/all_to_all | solution.py:439
  146.7 23.9 %all-to-all-start.2 = ((bf16[16,192,128]{2,1,0:T(8,128)(2,1)}), bf16[16,192,128]{2,1,0:T(8,128)(2,1)}, u32[]{:S(2)}, u32[]{:S(2)}) async-start(bf16[16,192,128]{2,1,0:T(8,128)(2,1)} %get-tuple-element.18.ctx_ref), calls=%async_computation.2 | async-start | bytes 1572864 | tf_op jit(solution)/shard_map/all_to_all | solution.py:450
  170.7 31.4 %all-to-all-start.3 = ((bf16[16,448,128]{2,1,0:T(8,128)(2,1)}), bf16[16,448,128]{2,1,0:T(8,128)(2,1)S(1)}, u32[]{:S(2)}, u32[]{:S(2)}) async-start(bf16[16,448,128]{2,1,0:T(8,128)(2,1)} %attend_back.1), calls=%async_computation.3 | async-start | bytes 3670016 | tf_op jit(solution)/shard_map/all_to_all | solution.py:466
  177.8 86.1 %reduce-scatter.2.cloned.1.call-start = ((), (), s32[]{:S(2)}) async-start(), calls=%async_computation.8 | async-start | bytes 7077888 | tf_op jit(solution)/shard_map/reduce_scatter | solution.py:501
  181.1 3.7 %copy-start.1 = (bf16[3,128,2048]{2,1,0:T(8,128)(2,1)S(1)}, bf16[3,128,2048]{2,1,0:T(8,128)(2,1)}, u32[]{:S(2)}) copy-start(bf16[3,128,2048]{2,1,0:T(8,128)(2,1)} %param.14) | copy-start | bytes 4718596
  181.1 10.7 %collective-permute-start = (bf16[1024,384]{1,0:T(8,128)(2,1)}, bf16[1024,384]{1,0:T(8,128)(2,1)}, u32[]{:S(2)}, u32[]{:S(2)}) collective-permute-start(bf16[1024,384]{1,0:T(8,128)(2,1)} %bitcast.54), channel_id=1, source_target_pairs={{0,1},{1,0},{2,3},{3,2},{4,5},{5,4},{6,7},{7,6},{8,9},{9,8},{10,11... | collective-permute-start | bytes 2359304 | tf_op jit(solution)/shard_map/ppermute | solution.py:413
  182.2 1.2 copy-start.5
  183.4 1.1 copy-start.8
  183.4 1.1 copy-start.10
  184.5 7.4 %collective-permute-start.1 = (bf16[1024,384]{1,0:T(8,128)(2,1)}, bf16[1024,384]{1,0:T(8,128)(2,1)}, u32[]{:S(2)}, u32[]{:S(2)}) collective-permute-start(bf16[1024,384]{1,0:T(8,128)(2,1)} %pad_maximum_fusion.5), channel_id=1, source_target_pairs={{0,1},{1,0},{2,3},{3,2},{4,5},{5,4},{6,7},{7,6},{8,9},{9,8},{10,11... | collective-permute-start | bytes 2359304 | tf_op jit(solution)/shard_map/ppermute | solution.py:470
  189.0 2.9 copy-start.6
  189.0 2.9 copy-start.9
  189.0 2.9 copy-start.11
  189.0 2.9 copy-start.12
  202.6 1.8 copy-start.2
  210.6 0.7 copy-start.16
  210.6 1.8 copy-start.7
  216.6 4.6 %copy-start.3 = (bf16[384,2048]{1,0:T(8,128)(2,1)}, bf16[384,2048]{1,0:T(8,128)(2,1)S(1)}, u32[]{:S(2)}) copy-start(bf16[384,2048]{1,0:T(8,128)(2,1)S(1)} %fusion.11) | copy-start | bytes 4718596
  216.6 4.6 %copy-start.13 = (f32[24,2048]{1,0:T(8,128)S(1)}, f32[24,2048]{1,0:T(8,128)}, u32[]{:S(2)}) copy-start(f32[24,2048]{1,0:T(8,128)} %fusion.39) | copy-start | bytes 589828
  216.6 5.1 %copy-start.15 = (f32[2048]{0:T(1024)S(1)}, f32[2048]{0:T(1024)}, u32[]{:S(2)}) copy-start(f32[2048]{0:T(1024)} %param.21) | copy-start | bytes 24580
  216.6 31.9 %all-to-all-start.4 = ((bf16[16,64,1024]{2,1,0:T(8,128)(2,1)}), bf16[16,64,1024]{2,1,0:T(8,128)(2,1)}, u32[]{:S(2)}, u32[]{:S(2)}) async-start(bf16[16,64,1024]{2,1,0:T(8,128)(2,1)} %bitcast.194), calls=%async_computation.5 | async-start | bytes 4194304 | tf_op jit(solution)/shard_map/all_to_all | solution.py:493
  221.2 1.3 copy-start.4
  266.1 21.2 %all-to-all-start.5 = ((bf16[16,16,1664]{2,1,0:T(8,128)(2,1)}), bf16[16,16,1664]{2,1,0:T(8,128)(2,1)S(1)}, u32[]{:S(2)}, u32[]{:S(2)}) async-start(bf16[16,16,1664]{2,1,0:T(8,128)(2,1)} %pad_maximum_fusion.2), calls=%async_computation.6 | async-start | bytes 1703936 | tf_op jit(solution)/shard_map/all_to_all | solution.py:521
  275.0 7.1 %collective-permute-start.4 = (f32[16,1024]{1,0:T(8,128)S(1)}, f32[16,1024]{1,0:T(8,128)S(1)}, u32[]{:S(2)}, u32[]{:S(2)}) collective-permute-start(f32[16,1024]{1,0:T(8,128)S(1)} %get-tuple-element.70), channel_id=1, source_target_pairs={{0,6},{2,0},{4,2},{6,4},{1,7},{3,1},{5,3},{7,5},{8,14},{10,8},{12,... | collective-permute-start | bytes 196616 | tf_op jit(solution)/shard_map/ppermute | solution.py:510
  277.5 5.9 %collective-permute-start.3 = (f32[16,1024]{1,0:T(8,128)S(1)}, f32[16,1024]{1,0:T(8,128)S(1)}, u32[]{:S(2)}, u32[]{:S(2)}) collective-permute-start(f32[16,1024]{1,0:T(8,128)S(1)} %get-tuple-element.71), channel_id=1, source_target_pairs={{0,4},{2,6},{4,0},{6,2},{1,5},{3,7},{5,1},{7,3},{8,12},{10,14},{12... | collective-permute-start | bytes 196616 | tf_op jit(solution)/shard_map/ppermute | solution.py:510
  277.5 6.2 %collective-permute-start.2 = (f32[16,1024]{1,0:T(8,128)S(1)}, f32[16,1024]{1,0:T(8,128)S(1)}, u32[]{:S(2)}, u32[]{:S(2)}) collective-permute-start(f32[16,1024]{1,0:T(8,128)S(1)} %get-tuple-element.69), channel_id=1, source_target_pairs={{0,2},{2,4},{4,6},{6,0},{1,3},{3,5},{5,7},{7,1},{8,10},{10,12},{12... | collective-permute-start | bytes 196616 | tf_op jit(solution)/shard_map/ppermute | solution.py:510
Sparse Core Ops, SparseCore 0:
  11.7 74.0 all-gather.1
  210.7 53.2 reduce-scatter.1
